TPU v7x, 256 devices: a whole 4x4x8 slice. The times are simulated.
256 devices in a mesh: band: 64 (over z, x_lo, y), pc: 4 (over x_hi, core).
Axes of the slice: x: 4 (x_hi: 2, x_lo: 2; x = x_hi * 2 + x_lo), y: 4, z: 8, core: 2. Of those that a mesh axis runs over, the one named last changes fastest.
Arguments:
- planes: bfloat16 [3, 256, 256, 256], P(None, 'band', 'pc'), may hold values from -15 to 15
- cotangent: bfloat16 [3, 256, 256, 256], P(None, 'band', 'pc'), may hold values from -6 to 6
- conv_weight: bfloat16 [9, 256, 256], P(None, 'pc'), may hold values from -0.125 to 0.125
- context_gain: bfloat16 [256], P('pc'), may hold values from 0.5 to 1.5
- step_index: int32 [1], replicated, may hold values from 0 to 999
Outputs:
- block_out: bfloat16 [3, 256, 256, 256], P(None, 'band', 'pc')
- input_grad: bfloat16 [3, 256, 256, 256], P(None, 'band', 'pc')
- weight_grad: float32 [9, 256, 256], P(None, 'pc', 'band')
All inputs are finite; a program needn't handle non-finite values.
Results may differ from a plain program's by a relative error of at most 0.0027.
The roundings to bfloat16 on the way count: a program that leaves them out, or rounds other values in their place, can miss the bound.
Values may be sent and summed in bfloat16 or wider, within the bound.
A program may use at most 64 MiB of HBM per device.

v0:
```python
import math

import jax
import jax.numpy as jnp
from jax import lax
from jax.sharding import PartitionSpec as P

C = 256


def with_halo(block, sides, width):
    for axis, dim in sides:
        count = lax.axis_size(axis)
        forward = [(i, i + 1) for i in range(count - 1)]
        backward = [(target, source) for source, target in forward]
        low = lax.ppermute(
            lax.slice_in_dim(block, block.shape[dim] - width, None, axis=dim), axis, forward
        )
        high = lax.ppermute(lax.slice_in_dim(block, 0, width, axis=dim), axis, backward)
        block = jnp.concatenate([low, block, high], axis=dim)
    return block


def time_embed(step_index, channel_ids, channels):
    moment = step_index[0].astype(jnp.float32)
    frequency = jnp.exp(
        -math.log(10000.0) * (2 * (channel_ids // 2)).astype(jnp.float32) / channels
    )
    phase = moment * frequency
    return jnp.where(channel_ids % 2 == 0, jnp.sin(phase), jnp.cos(phase))


def pooled(values):
    col_sums = jnp.sum(values, axis=1)
    row_sums = jnp.sum(values, axis=3)
    totals = lax.psum(col_sums, "band")
    row_sums_all = lax.all_gather(row_sums[2], "band", axis=0, tiled=True)
    return (totals, row_sums, row_sums_all)


def context(values, first_row, side_cells):
    totals, row_sums, row_sums_all = pooled(values)
    row_count = values.shape[1]
    own_columns = lax.dynamic_slice_in_dim(totals[0], first_row, row_count, 1)
    plane_one = row_sums[1][:, :, None] + jnp.transpose(row_sums_all)[None]
    plane_two = row_sums[0][:, :, None] + totals[2][None]
    plane_three = jnp.transpose(own_columns)[:, :, None] + totals[1][None]
    return jnp.stack([plane_one, plane_two, plane_three]) / side_cells


def convolve(values, weight, row_count, col_count):
    total = jnp.zeros((3, row_count, weight.shape[1], col_count), jnp.float32)
    for row_tap in range(3):
        for col_tap in range(3):
            window = values[:, row_tap : row_tap + row_count, :, col_tap : col_tap + col_count]
            total = total + jnp.einsum(
                "oc,kicj->kioj",
                weight[3 * row_tap + col_tap],
                window,
                preferred_element_type=jnp.float32,
            )
    return total


def transposed(values, weight, row_count, col_count):
    total = jnp.zeros((3, row_count, weight.shape[2], col_count), jnp.float32)
    for row_tap in range(3):
        for col_tap in range(3):
            window = values[
                :, 2 - row_tap : 2 - row_tap + row_count, :, 2 - col_tap : 2 - col_tap + col_count
            ]
            total = total + jnp.einsum(
                "oc,kioj->kicj",
                weight[3 * row_tap + col_tap],
                window,
                preferred_element_type=jnp.float32,
            )
    return total


def on_device(planes, cotangent, conv_weight, context_gain, step_index):
    row_count = planes.shape[1]
    local_channels = planes.shape[2]
    col_count = planes.shape[3]
    side_cells = row_count * lax.axis_size("band")
    first_row = lax.axis_index("band") * row_count
    whole = lax.all_gather(planes, "pc", axis=2, tiled=True)
    gathered = with_halo(whole, (("band", 1),), 1)
    padded = jnp.pad(gathered, ((0, 0), (0, 0), (0, 0), (1, 1)))
    inputs = planes.astype(jnp.float32)
    gain_vec = context_gain.astype(jnp.float32)[None, None, :, None]
    channel_ids = lax.axis_index("pc") * local_channels + jnp.arange(
        local_channels, dtype=jnp.int32
    )
    time_vec = time_embed(step_index, channel_ids, C)[None, None, :, None]
    pre_act = (
        convolve(padded, conv_weight, row_count, col_count)
        + gain_vec * context(inputs, first_row, side_cells)
        + time_vec
    )
    block_out = (inputs + jax.nn.silu(pre_act)).astype(jnp.bfloat16)
    sigma_z = jax.nn.sigmoid(pre_act)
    grad_z = (cotangent.astype(jnp.float32) * sigma_z * (1.0 + pre_act * (1.0 - sigma_z))).astype(
        jnp.bfloat16
    )
    grad_rim = with_halo(grad_z, (("band", 1),), 1)
    grad_rim = jnp.pad(grad_rim, ((0, 0), (0, 0), (0, 0), (1, 1)))
    all_grads, all_weights = (
        lax.all_gather(grad_rim, "pc", axis=2, tiled=True),
        lax.all_gather(conv_weight, "pc", axis=1, tiled=True),
    )
    own_weights = lax.dynamic_slice_in_dim(
        all_weights, lax.axis_index("pc") * local_channels, local_channels, 2
    )
    conv_back = transposed(all_grads, own_weights, row_count, col_count)
    context_back = context(gain_vec * grad_z.astype(jnp.float32), first_row, side_cells)
    input_grad = (cotangent.astype(jnp.float32) + conv_back + context_back).astype(jnp.bfloat16)
    weight_terms = []
    for row_tap in range(3):
        for col_tap in range(3):
            window = padded[:, row_tap : row_tap + row_count, :, col_tap : col_tap + col_count]
            weight_terms.append(
                jnp.einsum("kioj,kicj->oc", grad_z, window, preferred_element_type=jnp.float32)
            )
    weight_grad = lax.psum_scatter(jnp.stack(weight_terms), "band", scatter_dimension=2, tiled=True)
    return (block_out, input_grad, weight_grad)


def solution(mesh):
    in_specs = (
        P(None, "band", "pc", None),
        P(None, "band", "pc", None),
        P(None, "pc", None),
        P("pc"),
        P(),
    )
    out_specs = (P(None, "band", "pc", None), P(None, "band", "pc", None), P(None, "pc", "band"))
    return jax.shard_map(
        on_device, mesh=mesh, in_specs=in_specs, out_specs=out_specs, check_vma=False
    )
```

profile of v0, /device:TPU:2, one launch (start us, length us, event | category | flops | bytes accessed | tf_op | source)
XLA Modules:
  0.0 1473.8 jit_solution(5976371227544056289)
XLA Ops:
  8.1 1.9 convert_reduce_fusion.1
  10.0 0.5 all-gather.6.cloned.1.call-update
  10.6 152.1 %all-gather = f32[1,256,64]{2,0,1:T(1,128)S(1)} all-gather(f32[1,4,64]{2,0,1:T(1,128)S(1)} %bitcast.261), channel_id=2, replica_groups=mesh['band'=64,'pc'=4] {'band'}, dimensions={1}, use_global_device_ids=true | all-gather | bytes 66560 | tf_op jit(solution)/shard_map/all_gather | solution.py:37
  162.7 0.1 copy.82
  163.4 0.7 convert_element_type.40
  164.2 392.6 %all-reduce.5.cloned.1.call-done = f32[3,64,256]{2,1,0:T(8,128)} async-done(((f32[3,64,256]{2,1,0:T(8,128)}), f32[3,64,256]{2,1,0:T(8,128)}) %all-reduce.5.cloned.1.call-update) | async-done | bytes 196624 | tf_op jit(solution)/shard_map/psum | solution.py:36
  556.8 0.9 slice_bitcast_fusion.3
  557.7 0.1 constant_dynamic-slice_fusion.1
  557.9 0.1 broadcast_add_fusion.3
  558.1 1.3 fusion.203
  559.4 1.9 collective-permute-start
  561.3 6.0 collective-permute-start.1
  567.3 0.1 broadcast_add_fusion.4
  567.5 0.4 fusion.159
  567.8 4.3 collective-permute-done
  572.2 1.5 collective-permute-done.1
  573.7 2.4 fusion.5
  576.0 0.4 fusion.161
  576.4 0.7 fusion.163
  577.1 0.7 fusion.152
  577.8 0.4 fusion.156
  578.2 2.9 fusion.202
  581.1 0.3 pad_maximum_fusion.1
  581.4 0.4 fusion.165
  581.8 0.4 fusion.154
  582.2 0.5 fusion.81
  582.7 0.5 copy-done.2
  583.2 0.1 copy-done.4
  583.3 2.6 fusion.151
  585.9 0.6 fusion.91
  586.5 0.6 fusion.97
  587.0 0.6 fusion.103
  587.6 0.6 fusion.109
  588.2 0.6 fusion.115
  588.8 0.6 fusion.121
  589.4 0.6 fusion.127
  590.0 0.6 fusion.133
  590.7 0.6 fusion.139
  591.3 2.5 copy.106
  593.9 0.5 all-gather.10.cloned.1.call-update
  594.5 1.9 collective-permute-start.2
  596.4 6.5 collective-permute-start.3
  602.9 0.7 collective-permute-done.2
  603.6 1.5 collective-permute-done.3
  605.1 1.4 fusion.146
  606.5 144.9 %all-gather.1 = f32[1,256,64]{2,0,1:T(1,128)S(1)} all-gather(f32[1,4,64]{2,0,1:T(1,128)S(1)} %bitcast.262), channel_id=3, replica_groups=mesh['band'=64,'pc'=4] {'band'}, dimensions={1}, use_global_device_ids=true | all-gather | bytes 66560 | tf_op jit(solution)/shard_map/all_gather | solution.py:37
  751.4 0.1 copy.86
  751.5 0.1 broadcast_add_fusion.2
  751.6 386.6 %all-reduce.7.cloned.1.call-done = f32[3,64,256]{2,1,0:T(8,128)} async-done(((f32[3,64,256]{2,1,0:T(8,128)}), f32[3,64,256]{2,1,0:T(8,128)}) %all-reduce.7.cloned.1.call-update) | async-done | bytes 196624 | tf_op jit(solution)/shard_map/psum | solution.py:36
  1138.2 0.9 slice_bitcast_fusion.1
  1139.1 0.1 constant_dynamic-slice_fusion
  1139.3 0.1 broadcast_add_fusion.1
  1139.4 0.1 broadcast_add_fusion
  1139.5 309.4 %reduce-scatter.2.cloned.1.call-done = f32[9,64,4]{1,0,2:T(8,128)} async-done(((f32[9,64,256]{1,0,2:T(8,128)}), f32[9,64,4]{1,0,2:T(8,128)}) %reduce-scatter.2.cloned.1.call-update) | async-done | bytes 9232 | tf_op jit(solution)/shard_map/reduce_scatter | solution.py:125
  1448.9 1.4 copy.107
  1450.3 2.6 fusion.11
  1452.8 1.9 fusion.13
  1454.8 1.6 fusion.15
  1456.4 1.6 fusion.17
  1458.0 1.3 fusion.19
  1459.3 1.6 fusion.21
  1460.9 1.6 fusion.9
  1462.5 1.3 fusion.7
  1463.9 2.6 fusion.85
  (29 shorter events, 0.6 us)
Async XLA Ops:
  8.0 156.1 %copy-start.5 = (bf16[64]{0:T(256)(128)(2,1)S(1)}, bf16[64]{0:T(256)(128)(2,1)}, u32[]{:S(2)}) copy-start(bf16[64]{0:T(256)(128)(2,1)} %param.8) | copy-start | bytes 388
  8.0 548.8 %all-reduce.5.cloned.1.call-start = ((), (), s32[]{:S(2)}) async-start(), calls=%async_computation.2 | async-start | bytes 393216 | tf_op jit(solution)/shard_map/psum | solution.py:36
  9.9 548.1 %all-gather.6.cloned.1.call-start = ((), (), s32[]{:S(2)}) async-start(), calls=%async_computation.1 | async-start | bytes 1966080 | tf_op jit(solution)/shard_map/all_gather | solution.py:87
  10.5 1127.7 %all-reduce.7.cloned.1.call-start = ((), (), s32[]{:S(2)}) async-start(), calls=%async_computation.5 | async-start | bytes 393216 | tf_op jit(solution)/shard_map/psum | solution.py:36
  162.7 404.7 %copy-start.3 = (bf16[9,64,256]{2,1,0:T(8,128)(2,1)S(1)}, bf16[9,64,256]{2,1,0:T(8,128)(2,1)}, u32[]{:S(2)}) copy-start(bf16[9,64,256]{2,1,0:T(8,128)(2,1)} %param.7) | copy-start | bytes 884740
  558.1 9.4 copy-start.1
  559.4 12.8 collective-permute-start
  561.3 12.4 collective-permute-start.1
  582.2 1.0 copy-start.2
  582.2 1.1 copy-start.4
  590.7 858.2 %reduce-scatter.2.cloned.1.call-start = ((), (), s32[]{:S(2)}) async-start(), calls=%async_computation.6 | async-start | bytes 2129920 | tf_op jit(solution)/shard_map/reduce_scatter | solution.py:125
  593.8 856.5 %all-gather.10.cloned.1.call-start = ((), (), s32[]{:S(2)}) async-start(), calls=%async_computation.4 | async-start | bytes 1474560 | tf_op jit(solution)/shard_map/all_gather | solution.py:110
  594.4 855.9 %all-gather.8.cloned.1.call-start = ((), (), s32[]{:S(2)}) async-start(), calls=%async_computation.3 | async-start | bytes 4423680 | tf_op jit(solution)/shard_map/all_gather | solution.py:109
  594.5 9.1 collective-permute-start.2
  596.4 8.7 collective-permute-start.3
  1450.3 4.5 copy-start
Sparse Core Ops, SparseCore 0:
  12.0 544.7 all-reduce.4
  590.8 547.3 all-reduce.6
  1140.7 308.1 reduce-scatter.1
Sparse Core Ops, SparseCore 1:
  12.4 28.3 all-gather.5
  596.2 24.3 all-gather.9
  622.5 36.8 all-gather.7
where the time goes:
time: 1480 us; the launch traced here: 1470 us
  waiting for transfers between devices  1100 us (74%)
  blocking collectives  297 us (20%)
  matrix products  27.9 us (2%)
  starting transfers between devices  16.6 us (1%)
  between operations  16.4 us (1%)
    psum x2, waiting for transfers between devices, pooled(): totals = lax.psum(col_sums, 'band')  779 us
    reduce_scatter x1, waiting for transfers between devices, on_device(): lax.psum_scatter(jnp.stack(weight_terms), 'band', scatter_dimension=2, ti...  309 us
    all_gather x2, blocking collectives, pooled(): row_sums_all = lax.all_gather(row_sums[2], 'band', axis=0, tiled=True)  297 us
  transfers between devices with their start and end apart: 10, of which 7 were waited for; matrix products, arithmetic and copies ran while one was open for 1% of the time, Pallas kernels for 0%

commit v1 on v0

v1 whole, which is shorter than its diff:
```python
import math

import jax
import jax.numpy as jnp
from jax import lax
from jax.experimental import pallas as pl
from jax.experimental.pallas import tpu as pltpu
from jax.sharding import PartitionSpec as P

C = 256
MESH = pl.DeviceIdType.MESH
BANDS = 64
F32 = jnp.float32
BF16 = jnp.bfloat16


def time_embed(step_index, channel_ids, channels):
    moment = step_index[0].astype(jnp.float32)
    frequency = jnp.exp(
        -math.log(10000.0) * (2 * (channel_ids // 2)).astype(jnp.float32) / channels
    )
    phase = moment * frequency
    return jnp.where(channel_ids % 2 == 0, jnp.sin(phase), jnp.cos(phase))


def shifted(values, step):
    if step == 0:
        return values
    columns = lax.broadcasted_iota(jnp.int32, values.shape, 1)
    width = values.shape[1]
    rolled = pltpu.roll(values, step % width, 1)
    edge = 0 if step == 1 else width - 1
    return jnp.where(columns == edge, 0.0, rolled)


def kernel(
    planes, cotangent, weights, gain, time_vec,
    block_out, input_grad, weight_grad,
    rows, cot, wf, wa, wb, pre, stacks, out_a, out_b,
    sums, row_sums, ra, av, rb, gb, gc,
    wacc, wsend, rz, rv, rm,
    load_sem, send_sem, recv_sem, ar_send, ar_recv, w_send, w_recv, wg_send, wg_recv, store_sem,
):
    b = lax.axis_index("band")
    p = lax.axis_index("pc")
    z, m = b // 8, b % 8
    h, k = p // 2, p % 2
    across = (b, (1 - h) * 2 + k)
    beside = (b, h * 2 + (1 - k))
    above, below = (b - 1, p), (b + 1, p)
    has_above, has_below = b > 0, b < BANDS - 1

    def m_peer(step):
        return (z * 8 + (m + step) % 8, p)

    def z_peer(step):
        return (((z + step) % 8) * 8 + m, p)

    def load(number, src, dst):
        return pltpu.make_async_copy(src, dst, load_sem.at[number])

    loads = [load(i, planes.at[i], rows.at[0, i, pl.ds(1, 4), h, k]) for i in range(3)]
    loads.append(load(3, cotangent, cot))
    for tap_row in range(3):
        for tap_col in range(3):
            loads.append(
                load(
                    4 + 3 * tap_row + tap_col,
                    weights.at[3 * tap_row + tap_col],
                    wf.at[pl.ds(tap_col * 64, 64), pl.ds(tap_row * 256, 256)],
                )
            )
    half = pl.multiple_of(h * 128, 128)
    other_half = pl.multiple_of((1 - h) * 128, 128)
    loads.append(load(13, weights.at[:, :, pl.ds(half, 128)], wa.at[:, h, k]))
    for copy in loads:
        copy.start()

    barrier = pltpu.get_barrier_semaphore()
    for step in range(1, 8):
        pl.semaphore_signal(barrier, inc=1, device_id=m_peer(step), device_id_type=MESH)
        pl.semaphore_signal(barrier, inc=1, device_id=z_peer(step), device_id_type=MESH)
    pl.semaphore_signal(barrier, inc=1, device_id=across, device_id_type=MESH)
    pl.semaphore_signal(barrier, inc=1, device_id=beside, device_id_type=MESH)
    far_above = jnp.logical_and(m == 0, has_above)
    far_below = jnp.logical_and(m == 7, has_below)

    @pl.when(far_above)
    def _():
        pl.semaphore_signal(barrier, inc=1, device_id=above, device_id_type=MESH)

    @pl.when(far_below)
    def _():
        pl.semaphore_signal(barrier, inc=1, device_id=below, device_id_type=MESH)

    pl.semaphore_wait(
        barrier, 16 + far_above.astype(jnp.int32) + far_below.astype(jnp.int32)
    )

    def piece(which, plane, kind, dst, src, target):
        return pltpu.make_async_remote_copy(
            src_ref=src,
            dst_ref=dst,
            send_sem=send_sem.at[which, plane, kind],
            recv_sem=recv_sem.at[which, plane, kind],
            device_id=target,
            device_id_type=MESH,
        )

    def incoming(which, plane, kind, dst, target=None):
        return piece(which, plane, kind, dst, dst, across if target is None else target)

    def send_own(which, plane, own=None):
        buf = rows.at[which, plane]
        body = buf.at[pl.ds(1, 4), h, k]
        src = body if own is None else own
        first = buf.at[1, h, k] if own is None else own.at[0]
        last = buf.at[4, h, k] if own is None else own.at[3]
        piece(which, plane, 0, body, src, across).start()

        @pl.when(has_above)
        def _():
            piece(which, plane, 2, buf.at[5, h, k], first, above).start()

        @pl.when(has_below)
        def _():
            piece(which, plane, 3, buf.at[0, h, k], last, below).start()

        piece(which, plane, 1, body, src, beside).start()

    def pass_on(which, plane):
        buf = rows.at[which, plane]
        body = buf.at[pl.ds(1, 4), 1 - h, k]
        incoming(which, plane, 0, body).wait_recv()

        @pl.when(has_above)
        def _():
            piece(which, plane, 5, buf.at[5, 1 - h, k], buf.at[1, 1 - h, k], above).start()

        @pl.when(has_below)
        def _():
            piece(which, plane, 6, buf.at[0, 1 - h, k], buf.at[4, 1 - h, k], below).start()

        piece(which, plane, 4, body, body, beside).start()

    def pass_rim(which, plane):
        buf = rows.at[which, plane]

        @pl.when(has_below)
        def _():
            incoming(which, plane, 2, buf.at[5, h, k]).wait_recv()
            incoming(which, plane, 5, buf.at[5, 1 - h, k]).wait_recv()
            piece(which, plane, 7, buf.at[5, :, k], buf.at[5, :, k], beside).start()

        @pl.when(has_above)
        def _():
            incoming(which, plane, 3, buf.at[0, h, k]).wait_recv()
            incoming(which, plane, 6, buf.at[0, 1 - h, k]).wait_recv()
            piece(which, plane, 8, buf.at[0, :, k], buf.at[0, :, k], beside).start()

    def arrive(which, plane):
        buf = rows.at[which, plane]
        incoming(which, plane, 1, buf.at[pl.ds(1, 4), h, 1 - k]).wait_recv()
        incoming(which, plane, 4, buf.at[pl.ds(1, 4), 1 - h, 1 - k]).wait_recv()

        @pl.when(has_below)
        def _():
            incoming(which, plane, 7, buf.at[5, :, 1 - k]).wait_recv()

        @pl.when(has_above)
        def _():
            incoming(which, plane, 8, buf.at[0, :, 1 - k]).wait_recv()

    def settle(which, plane):
        buf = rows.at[which, plane]
        body = buf.at[pl.ds(1, 4), h, k]
        for kind in (0, 1, 4):
            piece(which, plane, kind, body, body, across).wait_send()

        @pl.when(has_above)
        def _():
            for kind in (2, 5):
                piece(which, plane, kind, buf.at[5, h, k], buf.at[5, h, k], above).wait_send()
            piece(which, plane, 8, buf.at[0, :, k], buf.at[0, :, k], beside).wait_send()

        @pl.when(has_below)
        def _():
            for kind in (3, 6):
                piece(which, plane, kind, buf.at[0, h, k], buf.at[0, h, k], below).wait_send()
            piece(which, plane, 7, buf.at[5, :, k], buf.at[5, :, k], beside).wait_send()

    def ar_copy(which, stage, step, src, dst, target):
        return pltpu.make_async_remote_copy(
            src_ref=src,
            dst_ref=dst,
            send_sem=ar_send.at[which, stage, step - 1],
            recv_sem=ar_recv.at[which, stage, step - 1],
            device_id=target,
            device_id_type=MESH,
        )

    def ar_start(which):
        for step in range(1, 8):
            to = (m + step) % 8
            ar_copy(
                which, 0, step, sums.at[which, to], ra.at[which, m], m_peer(step)
            ).start()
        ra[which, m] = sums[which, m]

    def ar_second(which):
        for step in range(1, 8):
            ar_copy(which, 0, step, sums.at[which, 0], ra.at[which, (m + 8 - step) % 8], m_peer(step)).wait_recv()
        total = ra[which, 0]
        for i in range(1, 8):
            total = total + ra[which, i]
        av[which] = total
        for step in range(1, 8):
            to = (z + step) % 8
            ar_copy(which, 1, step, av.at[which, to], rb.at[which, z], z_peer(step)).start()
        rb[which, z] = av[which, z]

    def ar_third(which):
        for step in range(1, 8):
            ar_copy(which, 1, step, av.at[which, 0], rb.at[which, (z + 8 - step) % 8], z_peer(step)).wait_recv()
        total = rb[which, 0]
        for i in range(1, 8):
            total = total + rb[which, i]
        gb[which, z] = total
        for step in range(1, 8):
            ar_copy(which, 2, step, gb.at[which, z], gb.at[which, z], z_peer(step)).start()

    def ar_fourth(which):
        for step in range(1, 8):
            slot = gb.at[which, (z + 8 - step) % 8]
            ar_copy(which, 2, step, slot, slot, z_peer(step)).wait_recv()
        for step in range(1, 8):
            ar_copy(which, 3, step, gb.at[which], gc.at[which, m], m_peer(step)).start()
        gc[which, m] = gb[which]

    def ar_finish(which):
        for step in range(1, 8):
            slot = gc.at[which, (m + 8 - step) % 8]
            ar_copy(which, 3, step, slot, slot, m_peer(step)).wait_recv()

    def ar_settle(which):
        for step in range(1, 8):
            ar_copy(which, 0, step, sums.at[which, 0], ra.at[which, 0], m_peer(step)).wait_send()
            ar_copy(which, 1, step, av.at[which, 0], rb.at[which, 0], z_peer(step)).wait_send()
            ar_copy(which, 2, step, gb.at[which, 0], gb.at[which, 0], z_peer(step)).wait_send()
            ar_copy(which, 3, step, gb.at[which], gc.at[which, 0], m_peer(step)).wait_send()

    columns = lax.broadcasted_iota(jnp.int32, (64, 256), 1)

    def make_sums(which):
        for plane in range(3):
            total = None
            spread = jnp.zeros((64, 256), F32)
            for i in range(4):
                values = rows[which, plane, 1 + i, h, k].astype(F32)
                total = values if total is None else total + values
                row = jnp.sum(values, axis=1, keepdims=True)
                if plane < 2:
                    row_sums[which, plane, i] = row
                else:
                    spread = jnp.where(columns == b * 4 + i, row, spread)
            for side in range(2):
                lanes = slice(side * 128, side * 128 + 128)
                sums[which, :, plane * 2 + side] = total[:, lanes].reshape(8, 8, 128)
                if plane == 2:
                    sums[which, :, 6 + side] = spread[:, lanes].reshape(8, 8, 128)

    def totals(which, number):
        return jnp.concatenate(
            [gc[which, :, number * 2 + side].reshape(64, 128) for side in range(2)], axis=1
        )

    def context_row(which, plane, i, whole):
        if plane == 0:
            return row_sums[which, 1, i] + whole
        if plane == 1:
            return row_sums[which, 0, i] + whole
        own = jnp.sum(
            jnp.where(columns == b * 4 + i, totals(which, 0), 0.0), axis=1, keepdims=True
        )
        return own + whole

    whole_of = (3, 2, 1)

    for i in range(3):
        send_own(0, i, planes.at[i])
    for i in range(3):
        loads[i].wait()
    make_sums(0)
    ar_start(0)

    def w_copy(kind, src, dst, target):
        return pltpu.make_async_remote_copy(
            src_ref=src, dst_ref=dst, send_sem=w_send.at[kind], recv_sem=w_recv.at[kind],
            device_id=target, device_id_type=MESH,
        )

    w_copy(0, weights.at[:, :, pl.ds(other_half, 128)], wa.at[:, h, k], across).start()
    w_copy(1, weights.at[:, :, pl.ds(half, 128)], wa.at[:, h, k], beside).start()

    zero_row = jnp.zeros((2, 2, 64, 256), BF16)

    @pl.when(jnp.logical_not(has_above))
    def _():
        for which in range(2):
            for plane in range(3):
                rows[which, plane, 0] = zero_row

    @pl.when(jnp.logical_not(has_below))
    def _():
        for which in range(2):
            for plane in range(3):
                rows[which, plane, 5] = zero_row

    for copy in loads[3:]:
        copy.wait()
    for plane in range(3):
        pass_on(0, plane)
    ar_second(0)
    for plane in range(3):
        pass_rim(0, plane)
    ar_third(0)

    def convolve(which, plane, matrix, back):
        def one(i, carry):
            slab = rows[which, plane, pl.ds(i, 3)].reshape(768, 256)
            parts = jnp.dot(matrix[...], slab, preferred_element_type=F32)
            signs = (-1, 0, 1) if back else (1, 0, -1)
            total = parts[64:128]
            for tap in (0, 2):
                total = total + shifted(parts[tap * 64 : tap * 64 + 64], signs[tap])
            pre[plane, i] = total
            return carry

        lax.fori_loop(0, 4, one, 0)

    arrive(0, 0)
    convolve(0, 0, wf, False)
    ar_fourth(0)
    arrive(0, 1)
    convolve(0, 1, wf, False)
    arrive(0, 2)
    convolve(0, 2, wf, False)

    arrived = wa.at[:, 1 - h, k]
    w_copy(0, arrived, arrived, across).wait_recv()
    w_copy(2, arrived, arrived, beside).start()

    ar_finish(0)
    gain_vec = gain[...]
    time_col = time_vec[...]
    for plane in range(3):
        whole = totals(0, whole_of[plane])

        def finish(i, carry):
            context = context_row(0, plane, i, whole) * (1.0 / 256.0)
            act = pre[plane, i] + gain_vec * context + time_col
            gate = jax.nn.sigmoid(act)
            values = rows[0, plane, 1 + i, h, k].astype(F32)
            out_a[plane, i] = (values + act * gate).astype(BF16)
            grad = cot[plane, i].astype(F32) * gate * (1.0 + act * (1.0 - gate))
            rows[1, plane, 1 + i, h, k] = grad.astype(BF16)
            return carry

        lax.fori_loop(0, 4, finish, 0)
        send_own(1, plane)
        pltpu.make_async_copy(out_a.at[plane], block_out.at[plane], store_sem.at[0, plane]).start()

    make_sums(1)
    ar_start(1)

    for plane in range(3):

        def stack(i, carry):
            grad = rows[1, plane, 1 + i, h, k].astype(F32)
            for tap in range(3):
                stacks[plane, i, pl.ds(tap * 64, 64)] = shifted(grad, tap - 1).astype(BF16)
            return carry

        lax.fori_loop(0, 4, stack, 0)

    for kind, dst in ((1, wa.at[:, h, 1 - k]), (2, wa.at[:, 1 - h, 1 - k])):
        w_copy(kind, dst, dst, beside).wait_recv()
    for tap_row in range(3):
        for tap_col in range(3):
            block = wa[3 * tap_row + tap_col].reshape(256, 128).astype(F32)
            turned = jnp.transpose(block)
            turned = jnp.where(k == 0, turned[:64], turned[64:])
            wb[pl.ds(tap_col * 64, 64), pl.ds((2 - tap_row) * 256, 256)] = turned.astype(BF16)

    def weight_terms(plane):
        grads = jnp.concatenate([stacks[plane, i] for i in range(4)], axis=1)

        for tap_row in range(3):
            window = jnp.concatenate(
                [rows[0, plane, tap_row + i].reshape(256, 256) for i in range(4)], axis=1
            )
            term = lax.dot_general(
                window, grads, (((1,), (1,)), ((), ())), preferred_element_type=F32
            )
            if plane == 0:
                wacc[tap_row] = term
            else:
                wacc[tap_row] += term

    def wg_copy(stage, step, src, dst, target):
        return pltpu.make_async_remote_copy(
            src_ref=src, dst_ref=dst,
            send_sem=wg_send.at[stage, step - 1], recv_sem=wg_recv.at[stage, step - 1],
            device_id=target, device_id_type=MESH,
        )

    weight_terms(0)
    pass_on(1, 0)
    ar_second(1)
    weight_terms(1)
    pass_on(1, 1)
    ar_third(1)
    weight_terms(2)
    pass_on(1, 2)
    for i in range(8):
        part = [wacc[tap_row, pl.ds(i * 32, 32), :] for tap_row in range(3)]
        part.append(jnp.zeros((32, 64), F32))
        wsend[i] = jnp.concatenate(part, axis=1)
    for step in range(1, 8):
        to = (z + step) % 8
        wg_copy(0, step, wsend.at[to], rz.at[z], z_peer(step)).start()
    rz[z] = wsend[z]
    ar_fourth(1)
    for plane in range(3):
        pass_rim(1, plane)
    for plane in range(3):
        arrive(1, plane)
        convolve(1, plane, wb, True)
    ar_finish(1)
    for plane in range(3):
        whole = totals(1, whole_of[plane])

        def finish_back(i, carry):
            context = context_row(1, plane, i, whole) * (1.0 / 256.0)
            grad = cot[plane, i].astype(F32) + pre[plane, i] + gain_vec * context
            out_b[plane, i] = grad.astype(BF16)
            return carry

        lax.fori_loop(0, 4, finish_back, 0)
        pltpu.make_async_copy(out_b.at[plane], input_grad.at[plane], store_sem.at[1, plane]).start()

    for step in range(1, 8):
        slot = rz.at[(z + 8 - step) % 8]
        wg_copy(0, step, slot, slot, z_peer(step)).wait_recv()
    total = rz[0]
    for i in range(1, 8):
        total = total + rz[i]
    rv[...] = total.reshape(4, 8, 640)
    for step in range(1, 8):
        to = (m + step) % 8
        wg_copy(1, step, rv.at[to // 2], rm.at[m], m_peer(step)).start()
    rm[m] = rv[m // 2]
    for step in range(1, 8):
        slot = rm.at[(m + 8 - step) % 8]
        wg_copy(1, step, slot, slot, m_peer(step)).wait_recv()
    total = rm[0]
    for i in range(1, 8):
        total = total + rm[i]
    total = jnp.where(m % 2 == 0, total[:4], total[4:])
    for tap in range(9):
        weight_grad[tap] = total[:, tap * 64 : tap * 64 + 64]

    for which in range(2):
        for plane in range(3):
            settle(which, plane)
        ar_settle(which)
    for kind in range(3):
        w_copy(kind, arrived, arrived, across).wait_send()
    for step in range(1, 8):
        wg_copy(0, step, wsend.at[0], rz.at[0], z_peer(step)).wait_send()
        wg_copy(1, step, rv.at[0], rm.at[0], m_peer(step)).wait_send()
    for plane in range(3):
        pltpu.make_async_copy(out_a.at[plane], block_out.at[plane], store_sem.at[0, plane]).wait()
        pltpu.make_async_copy(out_b.at[plane], input_grad.at[plane], store_sem.at[1, plane]).wait()


def on_device(planes, cotangent, conv_weight, context_gain, step_index):
    channel_ids = lax.axis_index("pc") * 64 + jnp.arange(64, dtype=jnp.int32)
    time_vec = time_embed(step_index, channel_ids, C)[:, None]
    gain = context_gain.astype(F32)[:, None]
    any_spec = pl.BlockSpec(memory_space=pl.ANY)
    vmem = pl.BlockSpec(memory_space=pltpu.VMEM)
    dma = pltpu.SemaphoreType.DMA
    block_out, input_grad, weight_grad = pl.pallas_call(
        kernel,
        out_shape=(
            jax.ShapeDtypeStruct((3, 4, 64, 256), BF16),
            jax.ShapeDtypeStruct((3, 4, 64, 256), BF16),
            jax.ShapeDtypeStruct((9, 4, 64), F32),
        ),
        in_specs=[any_spec, any_spec, any_spec, vmem, vmem],
        out_specs=(any_spec, any_spec, vmem),
        scratch_shapes=[
            pltpu.VMEM((2, 3, 6, 2, 2, 64, 256), BF16),
            pltpu.VMEM((3, 4, 64, 256), BF16),
            pltpu.VMEM((192, 768), BF16),
            pltpu.VMEM((9, 2, 2, 64, 128), BF16),
            pltpu.VMEM((192, 768), BF16),
            pltpu.VMEM((3, 4, 64, 256), F32),
            pltpu.VMEM((3, 4, 192, 256), BF16),
            pltpu.VMEM((3, 4, 64, 256), BF16),
            pltpu.VMEM((3, 4, 64, 256), BF16),
            pltpu.VMEM((2, 8, 8, 8, 128), F32),
            pltpu.VMEM((2, 2, 4, 64, 1), F32),
            pltpu.VMEM((2, 8, 8, 8, 128), F32),
            pltpu.VMEM((2, 8, 8, 128), F32),
            pltpu.VMEM((2, 8, 8, 128), F32),
            pltpu.VMEM((2, 8, 8, 128), F32),
            pltpu.VMEM((2, 8, 8, 8, 128), F32),
            pltpu.VMEM((3, 256, 192), F32),
            pltpu.VMEM((8, 32, 640), F32),
            pltpu.VMEM((8, 32, 640), F32),
            pltpu.VMEM((4, 8, 640), F32),
            pltpu.VMEM((8, 8, 640), F32),
            dma((14,)),
            dma((2, 3, 9)),
            dma((2, 3, 9)),
            dma((2, 4, 7)),
            dma((2, 4, 7)),
            dma((3,)),
            dma((3,)),
            dma((2, 7)),
            dma((2, 7)),
            dma((2, 3)),
        ],
        compiler_params=pltpu.CompilerParams(
            collective_id=0, has_side_effects=True, vmem_limit_bytes=48 * 1024 * 1024
        ),
        name="triplane",
    )(planes, cotangent, conv_weight, gain, time_vec)
    return block_out, input_grad, jnp.transpose(weight_grad, (0, 2, 1))


def solution(mesh):
    in_specs = (
        P(None, "band", "pc", None),
        P(None, "band", "pc", None),
        P(None, "pc", None),
        P("pc"),
        P(),
    )
    out_specs = (P(None, "band", "pc", None), P(None, "band", "pc", None), P(None, "pc", "band"))
    return jax.shard_map(
        on_device, mesh=mesh, in_specs=in_specs, out_specs=out_specs, check_vma=False
    )
```

time: 1480 us -> 89.6 us (0.06)
  waiting for transfers between devices: 1100 us -> 0 us
  blocking collectives: 297 us -> 0 us
  Pallas kernels: 0 us -> 80.6 us
  matrix products: 27.9 us -> 0 us
  starting transfers between devices: 16.6 us -> 0 us
  between operations: 16.4 us -> 1.3 us
    psum x2 -> x0, waiting for transfers between devices: 779 us -> none  [pooled(): totals = lax.psum(col_sums, 'band')]
    reduce_scatter x1 -> x0, waiting for transfers between devices: 309 us -> none  [on_device(): lax.psum_scatter(jnp.stack(weight_terms), 'band', scatter_dimension=2, ti...]
    all_gather x2 -> x0, blocking collectives: 297 us -> none  [pooled(): row_sums_all = lax.all_gather(row_sums[2], 'band', axis=0, tiled=True)]
    pallas_call x0 -> x1, Pallas kernels: none -> 80.6 us  [on_device(): pl.pallas_call(kernel, out_shape=(jax.ShapeDtypeStruct((3, 4, 64, 256), B...]
    dot_general x27 -> x0, matrix products: 27.9 us -> none  [the longest x9 16.2 us: transposed(): jnp.einsum('oc,kioj->kicj', weight[3 * row_tap + col_tap], window, prefer...]
    ppermute x4 -> x0, starting transfers between devices: 16.4 us -> none  [the longest x2 12.5 us: with_halo(): lax.ppermute(lax.slice_in_dim(block, 0, width, axis=dim), axis, backward)]
  transfers between devices with their start and end apart: 10 -> 0, of which waited for: 7 -> 0; matrix products, arithmetic and copies ran while one was open for 1% -> 0% of each run, Pallas kernels for 0% -> 0%
where the time goes in v1:
time: 89.6 us; the launch traced here: 87.9 us
  Pallas kernels  80.6 us (90%)
  local copies, waits for them, and re-layouts  5.8 us (6%)
  between operations  1.3 us (1%)
    pallas_call x1, Pallas kernels, on_device(): pl.pallas_call(kernel, out_shape=(jax.ShapeDtypeStruct((3, 4, 64, 256), B...  80.6 us
    unnamed x11, local copies, waits for them, and re-layouts  5.7 us

profile of v1, /device:TPU:2, one launch (start us, length us, event | category | flops | bytes accessed | tf_op | source)
XLA Modules:
  0.0 87.9 jit_solution(14805375551417290571)
XLA Ops:
  1.3 0.0 copy-start.3
  1.3 0.6 copy-done.3
  1.9 0.2 cosine_select_fusion.time_vec
  2.1 0.1 copy.8.gain
  2.2 0.0 copy-start
  2.2 1.0 %copy-done = bf16[3,4,64,256]{3,2,1,0:T(8,128)(2,1)S(1)} copy-done((bf16[3,4,64,256]{3,2,1,0:T(8,128)(2,1)S(1)}, bf16[3,4,64,256]{3,2,1,0:T(8,128)(2,1)}, u32[]{:S(2)}) %copy-start) | copy-done | bytes 393240
  3.2 0.0 copy-start.1
  3.2 1.0 %copy-done.1 = bf16[3,4,64,256]{3,2,1,0:T(8,128)(2,1)S(1)} copy-done((bf16[3,4,64,256]{3,2,1,0:T(8,128)(2,1)S(1)}, bf16[3,4,64,256]{3,2,1,0:T(8,128)(2,1)}, u32[]{:S(2)}) %copy-start.1) | copy-done | bytes 393240
  4.2 0.0 copy-start.2
  4.2 1.0 %copy-done.2 = bf16[9,64,256]{2,1,0:T(8,128)(2,1)S(1)} copy-done((bf16[9,64,256]{2,1,0:T(8,128)(2,1)S(1)}, bf16[9,64,256]{2,1,0:T(8,128)(2,1)}, u32[]{:S(2)}) %copy-start.2) | copy-done | bytes 294936
  5.2 80.6 %triplane.1 = (bf16[3,4,64,256]{3,2,1,0:T(8,128)(2,1)S(1)}, bf16[3,4,64,256]{3,2,1,0:T(8,128)(2,1)S(1)}, f32[9,4,64]{2,1,0:T(4,128)S(1)}) custom-call(bf16[3,4,64,256]{3,2,1,0:T(8,128)(2,1)S(1)} %copy-done, bf16[3,4,64,256]{3,2,1,0:T(8,128)(2,1)S(1)} %copy-done.1, bf16[9,64,256]{2,1,0:T(8,128)(2,1)S(1)} %copy-done.2, f32[64,1]{1,0:T(8,128)S(1)} %copy.8.gain, ...), custom_call_target="tpu_custom_call" | custom-call | tf_op jit(solution)/shard_map/triplane/pallas_call | solution.py:494
  85.8 0.7 copy.13
  86.6 0.7 copy.14
  87.3 0.6 copy.15
  (1 shorter events, 0.0 us)
Async XLA Ops:
  1.3 0.7 copy-start.3
  2.2 1.0 %copy-start = (bf16[3,4,64,256]{3,2,1,0:T(8,128)(2,1)S(1)}, bf16[3,4,64,256]{3,2,1,0:T(8,128)(2,1)}, u32[]{:S(2)}) copy-start(bf16[3,4,64,256]{3,2,1,0:T(8,128)(2,1)} %planes.1) | copy-start | bytes 1179652
  3.2 1.0 %copy-start.1 = (bf16[3,4,64,256]{3,2,1,0:T(8,128)(2,1)S(1)}, bf16[3,4,64,256]{3,2,1,0:T(8,128)(2,1)}, u32[]{:S(2)}) copy-start(bf16[3,4,64,256]{3,2,1,0:T(8,128)(2,1)} %cotangent.1) | copy-start | bytes 1179652
  4.2 1.0 %copy-start.2 = (bf16[9,64,256]{2,1,0:T(8,128)(2,1)S(1)}, bf16[9,64,256]{2,1,0:T(8,128)(2,1)}, u32[]{:S(2)}) copy-start(bf16[9,64,256]{2,1,0:T(8,128)(2,1)} %weights.1) | copy-start | bytes 884740

commit v2 on v1

v2 whole, which is shorter than its diff:
```python
import math

import jax
import jax.numpy as jnp
from jax import lax
from jax.experimental import pallas as pl
from jax.experimental.pallas import tpu as pltpu
from jax.sharding import PartitionSpec as P

C = 256
MESH = pl.DeviceIdType.MESH
BANDS = 64
VMEM_LIMIT = 60 * 1024 * 1024
WIRE = jnp.float32
F32 = jnp.float32
BF16 = jnp.bfloat16


def time_embed(step, channel_ids):
    frequency = jnp.exp(-math.log(10000.0) * (2 * (channel_ids // 2)).astype(F32) / C)
    phase = step.astype(F32) * frequency
    return jnp.where(channel_ids % 2 == 0, jnp.sin(phase), jnp.cos(phase))


def shifted(values, step):
    if step == 0:
        return values
    columns = lax.broadcasted_iota(jnp.int32, values.shape, 1)
    width = values.shape[1]
    rolled = pltpu.roll(values, step % width, 1)
    edge = 0 if step == 1 else width - 1
    return jnp.where(columns == edge, 0.0, rolled)


def kernel(
    planes, cotangent, weights, gain, step_index,
    block_out, input_grad, weight_grad,
    columns_of, rows, cot, wf, wa, wb, wo, pre, stacks, out_a, out_b,
    sums, row_sums, ra, rb, gc,
    wacc, wpack, wsend, rz, rv, rm,
    load_sem, send_sem, recv_sem, ar_send, ar_recv, w_send, w_recv, wg_send, wg_recv, store_sem,
):
    b = lax.axis_index("band")
    p = lax.axis_index("pc")
    z, m = b // 8, b % 8
    h, k = p // 2, p % 2
    across = (b, (1 - h) * 2 + k)
    beside = (b, h * 2 + (1 - k))
    above, below = (b - 1, p), (b + 1, p)
    has_above, has_below = b > 0, b < BANDS - 1

    y, xl, parity, zh = m % 4, m // 4, z % 2, z // 2

    def band_of(z_at, xl_at, y_at):
        return (z_at * 8 + xl_at * 4 + y_at, p)

    def g_place(step, sign=1):
        dy, dz = step % 4, step // 4
        return (y + 4 + sign * dy) % 4, (zh + 4 + sign * dz) % 4

    def g_peer(step):
        place, level = g_place(step)
        return band_of(level * 2 + parity, xl, place)

    def q_place(step):
        return (xl + step % 2) % 2, (parity + step // 2) % 2

    def q_peer(step):
        side, other = q_place(step)
        return band_of(zh * 2 + other, side, y)

    def m_peer(step):
        return (z * 8 + (m + step) % 8, p)

    def z_peer(step):
        return (((z + step) % 8) * 8 + m, p)

    def load(number, src, dst):
        return pltpu.make_async_copy(src, dst, load_sem.at[number])

    loads = [load(i, planes.at[i], rows.at[0, i, pl.ds(1, 4), h, k]) for i in range(3)]
    loads.append(load(3, cotangent, cot))
    for tap_row in range(3):
        for tap_col in range(3):
            loads.append(
                load(
                    4 + 3 * tap_row + tap_col,
                    weights.at[3 * tap_row + tap_col],
                    wf.at[pl.ds(tap_col * 64, 64), pl.ds(tap_row * 256, 256)],
                )
            )
    half = pl.multiple_of(h * 128, 128)
    other_half = pl.multiple_of((1 - h) * 128, 128)
    loads.append(load(13, weights.at[:, :, pl.ds(half, 128)], wa.at[:, h, k]))
    loads.append(load(14, weights.at[:, :, pl.ds(other_half, 128)], wo))
    for copy in loads:
        copy.start()

    barrier = pltpu.get_barrier_semaphore()

    def greet(target):
        pl.semaphore_signal(barrier, inc=1, device_id=target, device_id_type=MESH)

    for step in range(1, 8):
        greet(m_peer(step))
        greet(z_peer(step))
    for step in range(1, 16):
        if step % 4 and step // 4:
            greet(g_peer(step))
    greet(q_peer(3))
    greet(across)
    greet(beside)
    far_above = jnp.logical_and(m == 0, has_above)
    far_below = jnp.logical_and(m == 7, has_below)

    @pl.when(far_above)
    def _():
        greet(above)

    @pl.when(far_below)
    def _():
        greet(below)

    def meet():
        pl.semaphore_wait(
            barrier, 26 + far_above.astype(jnp.int32) + far_below.astype(jnp.int32)
        )

    def piece(which, plane, kind, dst, src, target):
        return pltpu.make_async_remote_copy(
            src_ref=src,
            dst_ref=dst,
            send_sem=send_sem.at[which, plane, kind],
            recv_sem=recv_sem.at[which, plane, kind],
            device_id=target,
            device_id_type=MESH,
        )

    def incoming(which, plane, kind, dst, target=None):
        return piece(which, plane, kind, dst, dst, across if target is None else target)

    def send_across(which, plane):
        buf = rows.at[which, plane]
        for kind, part in ((0, buf.at[1, h, k]), (1, buf.at[4, h, k]), (2, buf.at[pl.ds(2, 2), h, k])):
            piece(which, plane, kind, part, part, across).start()

    def send_near(which, plane):
        buf = rows.at[which, plane]
        body = buf.at[pl.ds(1, 4), h, k]

        @pl.when(has_above)
        def _():
            piece(which, plane, 3, buf.at[5, h, k], buf.at[1, h, k], above).start()

        @pl.when(has_below)
        def _():
            piece(which, plane, 4, buf.at[0, h, k], buf.at[4, h, k], below).start()

        piece(which, plane, 7, body, body, beside).start()

    def pass_edges(which, plane):
        buf = rows.at[which, plane]
        first, last = buf.at[1, 1 - h, k], buf.at[4, 1 - h, k]
        incoming(which, plane, 0, first).wait_recv()

        @pl.when(has_above)
        def _():
            piece(which, plane, 5, buf.at[5, 1 - h, k], first, above).start()

        incoming(which, plane, 1, last).wait_recv()

        @pl.when(has_below)
        def _():
            piece(which, plane, 6, buf.at[0, 1 - h, k], last, below).start()

    def pass_on(which, plane):
        buf = rows.at[which, plane]
        incoming(which, plane, 2, buf.at[pl.ds(2, 2), 1 - h, k]).wait_recv()
        body = buf.at[pl.ds(1, 4), 1 - h, k]
        piece(which, plane, 8, body, body, beside).start()

    def pass_rim(which, plane):
        buf = rows.at[which, plane]

        @pl.when(has_below)
        def _():
            incoming(which, plane, 3, buf.at[5, h, k]).wait_recv()
            incoming(which, plane, 5, buf.at[5, 1 - h, k]).wait_recv()
            piece(which, plane, 9, buf.at[5, :, k], buf.at[5, :, k], beside).start()

        @pl.when(has_above)
        def _():
            incoming(which, plane, 4, buf.at[0, h, k]).wait_recv()
            incoming(which, plane, 6, buf.at[0, 1 - h, k]).wait_recv()
            piece(which, plane, 10, buf.at[0, :, k], buf.at[0, :, k], beside).start()

    def arrive(which, plane):
        buf = rows.at[which, plane]
        incoming(which, plane, 7, buf.at[pl.ds(1, 4), h, 1 - k]).wait_recv()
        incoming(which, plane, 8, buf.at[pl.ds(1, 4), 1 - h, 1 - k]).wait_recv()

        @pl.when(has_below)
        def _():
            incoming(which, plane, 9, buf.at[5, :, 1 - k]).wait_recv()

        @pl.when(has_above)
        def _():
            incoming(which, plane, 10, buf.at[0, :, 1 - k]).wait_recv()

    def settle(which, plane):
        buf = rows.at[which, plane]
        one, body = buf.at[1, h, k], buf.at[pl.ds(1, 4), h, k]
        for kind in (0, 1):
            piece(which, plane, kind, one, one, across).wait_send()
        two = buf.at[pl.ds(2, 2), h, k]
        piece(which, plane, 2, two, two, across).wait_send()
        for kind in (7, 8):
            piece(which, plane, kind, body, body, beside).wait_send()

        @pl.when(has_above)
        def _():
            for kind in (3, 5):
                piece(which, plane, kind, one, one, above).wait_send()
            piece(which, plane, 10, buf.at[0, :, k], buf.at[0, :, k], beside).wait_send()

        @pl.when(has_below)
        def _():
            for kind in (4, 6):
                piece(which, plane, kind, one, one, below).wait_send()
            piece(which, plane, 9, buf.at[5, :, k], buf.at[5, :, k], beside).wait_send()

    def ar_copy(which, stage, step, src, dst, target):
        return pltpu.make_async_remote_copy(
            src_ref=src,
            dst_ref=dst,
            send_sem=ar_send.at[which, stage, step - 1],
            recv_sem=ar_recv.at[which, stage, step - 1],
            device_id=target,
            device_id_type=MESH,
        )

    def ar_start(which):
        for step in range(1, 16):
            place, level = g_place(step)
            ar_copy(
                which, 0, step, sums.at[which, place, level // 2, level % 2],
                ra.at[which, y, zh], g_peer(step),
            ).start()
        ra[which, y, zh] = sums[which, y, zh // 2, zh % 2]

    def ar_second(which):
        for step in range(1, 16):
            place, level = g_place(step, -1)
            slot = ra.at[which, place, level]
            ar_copy(which, 0, step, slot, slot, g_peer(step)).wait_recv()
        total = None
        for i in range(4):
            for j in range(4):
                total = ra[which, i, j] if total is None else total + ra[which, i, j]
        rb[which, xl, parity] = total
        for step in range(1, 4):
            slot = rb.at[which, xl, parity]
            ar_copy(which, 1, step, slot, slot, q_peer(step)).start()

    def ar_third(which):
        for step in range(1, 4):
            side, other = q_place(step)
            slot = rb.at[which, side, other]
            ar_copy(which, 1, step, slot, slot, q_peer(step)).wait_recv()
        total = (rb[which, 0, 0] + rb[which, 0, 1]) + (rb[which, 1, 0] + rb[which, 1, 1])
        gc[which, y, zh // 2, zh % 2] = total
        for step in range(1, 16):
            slot = gc.at[which, y, zh // 2, zh % 2]
            ar_copy(which, 2, step, slot, slot, g_peer(step)).start()

    def ar_finish(which):
        for step in range(1, 16):
            place, level = g_place(step, -1)
            slot = gc.at[which, place, level // 2, level % 2]
            ar_copy(which, 2, step, slot, slot, g_peer(step)).wait_recv()

    def ar_settle(which):
        slot = gc.at[which, 0, 0, 0]
        for step in range(1, 16):
            ar_copy(which, 0, step, slot, slot, g_peer(step)).wait_send()
            ar_copy(which, 2, step, slot, slot, g_peer(step)).wait_send()
        for step in range(1, 4):
            ar_copy(which, 1, step, slot, slot, q_peer(step)).wait_send()

    columns = lax.broadcasted_iota(jnp.int32, (64, 256), 1)

    def make_sums(which):
        for plane in range(3):
            total = None
            spread = jnp.zeros((64, 256), F32)
            for i in range(4):
                values = rows[which, plane, 1 + i, h, k].astype(F32)
                total = values if total is None else total + values
                row = jnp.sum(values, axis=1, keepdims=True)
                if plane < 2:
                    row_sums[which, plane, i] = row
                else:
                    spread = jnp.where(columns == b * 4 + i, row, spread)
            for side in range(2):
                lanes = slice(side * 128, side * 128 + 128)
                sums[which, :, :, side, plane] = total[:, lanes].reshape(4, 2, 8, 128)
                if plane == 2:
                    sums[which, :, :, side, 3] = spread[:, lanes].reshape(4, 2, 8, 128)

    def totals(which, number):
        return jnp.concatenate(
            [gc[which, :, :, side, number].reshape(64, 128) for side in range(2)], axis=1
        )

    def context_row(which, plane, i, whole):
        if plane == 0:
            return row_sums[which, 1, i] + whole
        if plane == 1:
            return row_sums[which, 0, i] + whole
        own = jnp.sum(
            jnp.where(columns == b * 4 + i, totals(which, 0), 0.0), axis=1, keepdims=True
        )
        return own + whole

    whole_of = (3, 2, 1)

    def w_copy(kind, src, dst, target):
        return pltpu.make_async_remote_copy(
            src_ref=src, dst_ref=dst, send_sem=w_send.at[kind], recv_sem=w_recv.at[kind],
            device_id=target, device_id_type=MESH,
        )

    def wg_copy(stage, step, src, dst, target):
        return pltpu.make_async_remote_copy(
            src_ref=src, dst_ref=dst,
            send_sem=wg_send.at[stage, step - 1], recv_sem=wg_recv.at[stage, step - 1],
            device_id=target, device_id_type=MESH,
        )

    def convolve(which, plane, matrix, back):
        def one(i, carry):
            slab = rows[which, plane, pl.ds(i, 3)].reshape(768, 256)
            parts = jnp.dot(matrix[...], slab, preferred_element_type=F32)
            signs = (-1, 0, 1) if back else (1, 0, -1)
            total = parts[64:128]
            for tap in (0, 2):
                total = total + shifted(parts[tap * 64 : tap * 64 + 64], signs[tap])
            pre[plane, i] = total
            return carry

        lax.fori_loop(0, 4, one, 0)

    def turn_weights():
        for tap_row in range(3):
            for tap_col in range(3):
                block = wa[3 * tap_row + tap_col].reshape(256, 128).astype(F32)
                turned = jnp.transpose(block)
                turned = jnp.where(k == 0, turned[:64], turned[64:])
                wb[pl.ds(tap_col * 64, 64), pl.ds((2 - tap_row) * 256, 256)] = turned.astype(BF16)

    def finish_plane(plane):
        whole = totals(0, whole_of[plane])
        gain_vec, time_col = columns_of[0], columns_of[1]

        def finish(i, carry):
            context = context_row(0, plane, i, whole) * (1.0 / 256.0)
            act = pre[plane, i] + gain_vec * context + time_col
            gate = jax.nn.sigmoid(act)
            values = rows[0, plane, 1 + i, h, k].astype(F32)
            out_a[plane, i] = (values + act * gate).astype(BF16)
            grad = cot[plane, i].astype(F32) * gate * (1.0 + act * (1.0 - gate))
            rows[1, plane, 1 + i, h, k] = grad.astype(BF16)
            return carry

        lax.fori_loop(0, 4, finish, 0)

    def stack_plane(plane):
        def stack(i, carry):
            grad = rows[1, plane, 1 + i, h, k].astype(F32)
            for tap in range(3):
                stacks[plane, i, pl.ds(tap * 64, 64)] = shifted(grad, tap - 1).astype(BF16)
            return carry

        lax.fori_loop(0, 4, stack, 0)

    def weight_terms(plane):
        grads = jnp.concatenate([stacks[plane, i] for i in range(4)], axis=1)
        for tap_row in range(3):
            window = jnp.concatenate(
                [rows[0, plane, tap_row + i].reshape(256, 256) for i in range(4)], axis=1
            )
            term = lax.dot_general(
                window, grads, (((1,), (1,)), ((), ())), preferred_element_type=F32
            )
            if plane == 0:
                wacc[tap_row] = term
            else:
                wacc[tap_row] += term

    def wg_pack():
        for i in range(8):
            part = [wacc[tap_row, pl.ds(i * 32, 32), :] for tap_row in range(3)]
            part.append(jnp.zeros((32, 64), F32))
            block = jnp.concatenate(part, axis=1)
            for j in range(8):
                wpack[j, pl.ds(i * 4, 4)] = block[j * 4 : j * 4 + 4]
        wsend[...] = wpack[...].astype(WIRE)

    def wg_start():
        for step in range(1, 8):
            wg_copy(0, step, wsend.at[(m + step) % 8], rz.at[m], m_peer(step)).start()
        rz[m] = wsend[m]

    def wg_second():
        for step in range(1, 8):
            slot = rz.at[(m + 8 - step) % 8]
            wg_copy(0, step, slot, slot, m_peer(step)).wait_recv()
        total = rz[0].astype(F32)
        for i in range(1, 8):
            total = total + rz[i].astype(F32)
        for i in range(8):
            rv[i] = total[i * 4 : i * 4 + 4]
        for step in range(1, 8):
            wg_copy(1, step, rv.at[(z + step) % 8], rm.at[z], z_peer(step)).start()
        rm[z] = rv[z]

    def wg_finish():
        for step in range(1, 8):
            slot = rm.at[(z + 8 - step) % 8]
            wg_copy(1, step, slot, slot, z_peer(step)).wait_recv()
        total = rm[0]
        for i in range(1, 8):
            total = total + rm[i]
        for tap in range(9):
            weight_grad[tap] = total[:, tap * 64 : tap * 64 + 64]

    def wg_settle():
        for step in range(1, 8):
            wg_copy(0, step, wsend.at[0], rz.at[0], m_peer(step)).wait_send()
            wg_copy(1, step, rv.at[0], rm.at[0], z_peer(step)).wait_send()

    def make_columns():
        ids = lax.broadcasted_iota(jnp.int32, (64, 128), 0) + p * 64
        columns_of[1] = time_embed(step_index[0], ids)[:, :1]
        across_lanes = jnp.broadcast_to(gain[...].astype(F32).reshape(1, 64), (64, 64))
        same = lax.broadcasted_iota(jnp.int32, (64, 64), 0) == lax.broadcasted_iota(
            jnp.int32, (64, 64), 1
        )
        columns_of[0] = jnp.sum(jnp.where(same, across_lanes, 0.0), axis=1, keepdims=True)

    def finish_back_plane(plane):
        whole = totals(1, whole_of[plane])
        gain_vec = columns_of[0]

        def finish_back(i, carry):
            context = context_row(1, plane, i, whole) * (1.0 / 256.0)
            grad = cot[plane, i].astype(F32) + pre[plane, i] + gain_vec * context
            out_b[plane, i] = grad.astype(BF16)
            return carry

        lax.fori_loop(0, 4, finish_back, 0)

    for i in range(3):
        loads[i].wait()
    make_sums(0)
    make_columns()
    zero_row = jnp.zeros((2, 2, 64, 256), BF16)

    @pl.when(jnp.logical_not(has_above))
    def _():
        for which in range(2):
            for plane in range(3):
                rows[which, plane, 0] = zero_row

    @pl.when(jnp.logical_not(has_below))
    def _():
        for which in range(2):
            for plane in range(3):
                rows[which, plane, 5] = zero_row

    meet()
    ar_start(0)
    send_across(0, 0)
    send_across(0, 1)
    for plane in range(3):
        send_near(0, plane)
    for copy in loads[3:]:
        copy.wait()
    w_copy(1, wa.at[:, h, k], wa.at[:, h, k], beside).start()
    pass_edges(0, 0)
    ar_second(0)
    send_across(0, 2)
    pass_on(0, 0)
    pass_edges(0, 1)
    pass_on(0, 1)
    pass_rim(0, 0)
    arrive(0, 0)
    convolve(0, 0, wf, False)
    ar_third(0)
    pass_edges(0, 2)
    pass_on(0, 2)
    w_copy(0, wo, wa.at[:, h, k], across).start()
    pass_rim(0, 1)
    arrive(0, 1)
    convolve(0, 1, wf, False)
    pass_rim(0, 2)
    arrive(0, 2)
    convolve(0, 2, wf, False)

    ar_finish(0)
    finish_plane(0)
    send_across(1, 0)
    finish_plane(1)
    send_across(1, 1)
    finish_plane(2)
    make_sums(1)
    ar_start(1)
    for plane in range(3):
        send_near(1, plane)
        pltpu.make_async_copy(out_a.at[plane], block_out.at[plane], store_sem.at[0, plane]).start()
    stack_plane(0)
    weight_terms(0)
    pass_edges(1, 0)
    stack_plane(1)
    weight_terms(1)
    pass_on(1, 0)
    pass_edges(1, 1)
    stack_plane(2)
    weight_terms(2)
    ar_second(1)
    send_across(1, 2)
    pass_on(1, 1)
    wg_pack()
    wg_start()
    pass_rim(1, 0)
    arrived = wa.at[:, 1 - h, k]
    w_copy(0, arrived, arrived, across).wait_recv()
    w_copy(2, arrived, arrived, beside).start()
    pass_edges(1, 2)
    ar_third(1)
    pass_on(1, 2)
    for kind, dst in ((1, wa.at[:, h, 1 - k]), (2, wa.at[:, 1 - h, 1 - k])):
        w_copy(kind, dst, dst, beside).wait_recv()
    turn_weights()
    pass_rim(1, 1)
    arrive(1, 0)
    convolve(1, 0, wb, True)
    pass_rim(1, 2)
    arrive(1, 1)
    convolve(1, 1, wb, True)
    wg_second()
    arrive(1, 2)
    convolve(1, 2, wb, True)
    ar_finish(1)
    for plane in range(3):
        finish_back_plane(plane)
        pltpu.make_async_copy(out_b.at[plane], input_grad.at[plane], store_sem.at[1, plane]).start()
    wg_finish()

    for which in range(2):
        for plane in range(3):
            settle(which, plane)
        ar_settle(which)
    w_copy(0, wo, wo, across).wait_send()
    for kind in (1, 2):
        w_copy(kind, arrived, arrived, beside).wait_send()
    wg_settle()
    for plane in range(3):
        pltpu.make_async_copy(out_a.at[plane], block_out.at[plane], store_sem.at[0, plane]).wait()
        pltpu.make_async_copy(out_b.at[plane], input_grad.at[plane], store_sem.at[1, plane]).wait()


def place(*refs):
    sources, targets, held, sems = refs[:3], refs[3:6], refs[6:9], refs[9]
    arriving = [pltpu.make_async_copy(sources[i], held[i], sems.at[0, i]) for i in range(3)]
    leaving = [pltpu.make_async_copy(held[i], targets[i], sems.at[1, i]) for i in range(3)]
    for copy in arriving:
        copy.start()
    for i in range(3):
        arriving[i].wait()
        leaving[i].start()
    for copy in leaving:
        copy.wait()


def on_device(planes, cotangent, conv_weight, context_gain, step_index):
    anywhere = pl.BlockSpec(memory_space=pl.ANY)
    hbm = pl.BlockSpec(memory_space=pltpu.HBM)
    vmem = pl.BlockSpec(memory_space=pltpu.VMEM)
    smem = pl.BlockSpec(memory_space=pltpu.SMEM)
    dma = pltpu.SemaphoreType.DMA
    shapes = (
        jax.ShapeDtypeStruct((3, 4, 64, 256), BF16),
        jax.ShapeDtypeStruct((3, 4, 64, 256), BF16),
        jax.ShapeDtypeStruct((9, 4, 64), F32),
    )
    results = pl.pallas_call(
        kernel,
        out_shape=shapes,
        in_specs=[hbm, hbm, hbm, vmem, smem],
        out_specs=(anywhere, anywhere, vmem),
        scratch_shapes=[
            pltpu.VMEM((2, 64, 1), F32),
            pltpu.VMEM((2, 3, 6, 2, 2, 64, 256), BF16),
            pltpu.VMEM((3, 4, 64, 256), BF16),
            pltpu.VMEM((192, 768), BF16),
            pltpu.VMEM((9, 2, 2, 64, 128), BF16),
            pltpu.VMEM((192, 768), BF16),
            pltpu.VMEM((9, 64, 128), BF16),
            pltpu.VMEM((3, 4, 64, 256), F32),
            pltpu.VMEM((3, 4, 192, 256), BF16),
            pltpu.VMEM((3, 4, 64, 256), BF16),
            pltpu.VMEM((3, 4, 64, 256), BF16),
            pltpu.VMEM((2, 4, 2, 2, 4, 8, 128), F32),
            pltpu.VMEM((2, 2, 4, 64, 1), F32),
            pltpu.VMEM((2, 4, 4, 4, 8, 128), F32),
            pltpu.VMEM((2, 2, 2, 4, 8, 128), F32),
            pltpu.VMEM((2, 4, 2, 2, 4, 8, 128), F32),
            pltpu.VMEM((3, 256, 192), F32),
            pltpu.VMEM((8, 32, 640), F32),
            pltpu.VMEM((8, 32, 640), WIRE),
            pltpu.VMEM((8, 32, 640), WIRE),
            pltpu.VMEM((8, 4, 640), F32),
            pltpu.VMEM((8, 4, 640), F32),
            dma((15,)),
            dma((2, 3, 11)),
            dma((2, 3, 11)),
            dma((2, 3, 15)),
            dma((2, 3, 15)),
            dma((3,)),
            dma((3,)),
            dma((2, 7)),
            dma((2, 7)),
            dma((2, 3)),
        ],
        compiler_params=pltpu.CompilerParams(
            collective_id=0, has_side_effects=True, vmem_limit_bytes=VMEM_LIMIT
        ),
        name="triplane",
    )(planes, cotangent, conv_weight, context_gain, step_index)
    block_out, input_grad, weight_grad = pl.pallas_call(
        place,
        out_shape=shapes,
        in_specs=[anywhere] * 3,
        out_specs=(hbm, hbm, hbm),
        scratch_shapes=[pltpu.VMEM(shape.shape, shape.dtype) for shape in shapes] + [dma((2, 3))],
        compiler_params=pltpu.CompilerParams(vmem_limit_bytes=VMEM_LIMIT),
        name="place",
    )(*results)
    return block_out, input_grad, jnp.transpose(weight_grad, (0, 2, 1))


def solution(mesh):
    in_specs = (
        P(None, "band", "pc", None),
        P(None, "band", "pc", None),
        P(None, "pc", None),
        P("pc"),
        P(),
    )
    out_specs = (P(None, "band", "pc", None), P(None, "band", "pc", None), P(None, "pc", "band"))
    return jax.shard_map(
        on_device, mesh=mesh, in_specs=in_specs, out_specs=out_specs, check_vma=False
    )
```

time: 89.6 us -> 74.5 us (0.83); the launches traced: 87.9 us -> 74 us
  Pallas kernels: 80.6 us -> 72.7 us
  local copies, waits for them, and re-layouts: 5.8 us -> 0 us
    pallas_call x1 -> x2, Pallas kernels: 80.6 us -> 72.7 us  [the longest x1 70.8 us: on_device(): pl.pallas_call(kernel, out_shape=shapes, in_specs=[hbm, hbm, hbm, vmem, s...]
    unnamed x11 -> x0, local copies, waits for them, and re-layouts: 5.7 us -> none
where the time goes in v2:
time: 74.5 us; the launch traced here: 74 us
  Pallas kernels  72.7 us (98%)
  between operations  1.29 us (2%)
    pallas_call x1, Pallas kernels, on_device(): pl.pallas_call(kernel, out_shape=shapes, in_specs=[hbm, hbm, hbm, vmem, s...  70.8 us
    pallas_call x1, Pallas kernels, on_device(): pl.pallas_call(place, out_shape=shapes, in_specs=[anywhere] * 3, out_spec...  1.93 us

profile of v2, /device:TPU:2, one launch (start us, length us, event | category | flops | bytes accessed | tf_op | source)
XLA Modules:
  0.0 74.0 jit_solution(5382971745630168239)
XLA Ops:
  1.3 70.8 %triplane.1 = (bf16[3,4,64,256]{3,2,1,0:T(8,128)(2,1)}, bf16[3,4,64,256]{3,2,1,0:T(8,128)(2,1)}, f32[9,4,64]{2,1,0:T(4,128)}) custom-call(bf16[3,4,64,256]{3,2,1,0:T(8,128)(2,1)} %planes.1, bf16[3,4,64,256]{3,2,1,0:T(8,128)(2,1)} %cotangent.1, bf16[9,64,256]{2,1,0:T(8,128)(2,1)} %weights.1, bf16[64]{0:T(256)(128)(2,1)} %gain.1, s32[1]{0:T(128)S(6)} %copy.8.step_index), custom_call_target="tpu_custom_call" | custom-call | tf_op jit(solution)/shard_map/triplane/pallas_call | solution.py:597
  72.0 1.9 %place.1 = (bf16[3,4,64,256]{3,2,1,0:T(8,128)(2,1)}, bf16[3,4,64,256]{3,2,1,0:T(8,128)(2,1)}, f32[9,4,64]{2,1,0:T(4,128)}) custom-call(bf16[3,4,64,256]{3,2,1,0:T(8,128)(2,1)} %get-tuple-element.9.refs_0_, bf16[3,4,64,256]{3,2,1,0:T(8,128)(2,1)} %get-tuple-element.10.refs_1_, f32[9,4,64]{2,1,0:T(4,128)} %get-tuple-element.11.refs_2_), custom_call_target="tpu_custom_call" | custom-call | tf_op jit(solution)/shard_map/place/pallas_call | solution.py:641

commit v3 on v2

--- a/solution.py
+++ b/solution.py
@@ -10,8 +10,7 @@
 C = 256
 MESH = pl.DeviceIdType.MESH
 BANDS = 64
-VMEM_LIMIT = 60 * 1024 * 1024
-WIRE = jnp.float32
+VMEM_LIMIT = 40 * 1024 * 1024
 F32 = jnp.float32
 BF16 = jnp.bfloat16
 
@@ -35,10 +34,10 @@
 def kernel(
     planes, cotangent, weights, gain, step_index,
     block_out, input_grad, weight_grad,
-    columns_of, rows, cot, wf, wa, wb, wo, pre, stacks, out_a, out_b,
+    columns_of, gain_row, rows, cot, wf, wa, wb, wo, pre, stacks,
     sums, row_sums, ra, rb, gc,
-    wacc, wpack, wsend, rz, rv, rm,
-    load_sem, send_sem, recv_sem, ar_send, ar_recv, w_send, w_recv, wg_send, wg_recv, store_sem,
+    wacc, wsend, rz, rv, rm,
+    load_sem, send_sem, recv_sem, ar_send, ar_recv, w_send, w_recv, wg_send, wg_recv,
 ):
     b = lax.axis_index("band")
     p = lax.axis_index("pc")
@@ -49,31 +48,17 @@
     above, below = (b - 1, p), (b + 1, p)
     has_above, has_below = b > 0, b < BANDS - 1
 
-    y, xl, parity, zh = m % 4, m // 4, z % 2, z // 2
-
-    def band_of(z_at, xl_at, y_at):
-        return (z_at * 8 + xl_at * 4 + y_at, p)
-
-    def g_place(step, sign=1):
-        dy, dz = step % 4, step // 4
-        return (y + 4 + sign * dy) % 4, (zh + 4 + sign * dz) % 4
+    parity = z % 2
+
+    def g_place(dm, dz):
+        return (m + dm) % 8, (parity + dz) % 2
 
     def g_peer(step):
-        place, level = g_place(step)
-        return band_of(level * 2 + parity, xl, place)
-
-    def q_place(step):
-        return (xl + step % 2) % 2, (parity + step // 2) % 2
+        place, side = g_place(step % 8, step // 8)
+        return ((z // 2 * 2 + side) * 8 + place, p)
 
     def q_peer(step):
-        side, other = q_place(step)
-        return band_of(zh * 2 + other, side, y)
-
-    def m_peer(step):
-        return (z * 8 + (m + step) % 8, p)
-
-    def z_peer(step):
-        return (((z + step) % 8) * 8 + m, p)
+        return (((z + 2 * step) % 8) * 8 + m, p)
 
     def load(number, src, dst):
         return pltpu.make_async_copy(src, dst, load_sem.at[number])
@@ -93,6 +78,8 @@
     other_half = pl.multiple_of((1 - h) * 128, 128)
     loads.append(load(13, weights.at[:, :, pl.ds(half, 128)], wa.at[:, h, k]))
     loads.append(load(14, weights.at[:, :, pl.ds(other_half, 128)], wo))
+    gain_load = load(15, gain, gain_row)
+    gain_load.start()
     for copy in loads:
         copy.start()
 
@@ -101,17 +88,14 @@
     def greet(target):
         pl.semaphore_signal(barrier, inc=1, device_id=target, device_id_type=MESH)
 
-    for step in range(1, 8):
-        greet(m_peer(step))
-        greet(z_peer(step))
+    for step in range(1, 4):
+        greet(q_peer(step))
     for step in range(1, 16):
-        if step % 4 and step // 4:
-            greet(g_peer(step))
-    greet(q_peer(3))
+        greet(g_peer(step))
     greet(across)
     greet(beside)
-    far_above = jnp.logical_and(m == 0, has_above)
-    far_below = jnp.logical_and(m == 7, has_below)
+    far_above = jnp.logical_and(jnp.logical_and(m == 0, parity == 0), has_above)
+    far_below = jnp.logical_and(jnp.logical_and(m == 7, parity == 1), has_below)
 
     @pl.when(far_above)
     def _():
@@ -123,7 +107,7 @@
 
     def meet():
         pl.semaphore_wait(
-            barrier, 26 + far_above.astype(jnp.int32) + far_below.astype(jnp.int32)
+            barrier, 20 + far_above.astype(jnp.int32) + far_below.astype(jnp.int32)
         )
 
     def piece(which, plane, kind, dst, src, target):
@@ -139,10 +123,14 @@
     def incoming(which, plane, kind, dst, target=None):
         return piece(which, plane, kind, dst, dst, across if target is None else target)
 
-    def send_across(which, plane):
+    def send_edges(which, plane):
         buf = rows.at[which, plane]
-        for kind, part in ((0, buf.at[1, h, k]), (1, buf.at[4, h, k]), (2, buf.at[pl.ds(2, 2), h, k])):
+        for kind, part in ((0, buf.at[1, h, k]), (1, buf.at[4, h, k])):
             piece(which, plane, kind, part, part, across).start()
+
+    def send_inner(which, plane):
+        part = rows.at[which, plane, pl.ds(2, 2), h, k]
+        piece(which, plane, 2, part, part, across).start()
 
     def send_near(which, plane):
         buf = rows.at[which, plane]
@@ -241,46 +229,46 @@
 
     def ar_start(which):
         for step in range(1, 16):
-            place, level = g_place(step)
+            place, side = g_place(step % 8, step // 8)
             ar_copy(
-                which, 0, step, sums.at[which, place, level // 2, level % 2],
-                ra.at[which, y, zh], g_peer(step),
+                which, 0, step, sums.at[which, place, side], ra.at[which, m, parity], g_peer(step)
             ).start()
-        ra[which, y, zh] = sums[which, y, zh // 2, zh % 2]
+        ra[which, m, parity] = sums[which, m, parity]
 
     def ar_second(which):
         for step in range(1, 16):
-            place, level = g_place(step, -1)
-            slot = ra.at[which, place, level]
+            place, side = g_place(-(step % 8) + 8, step // 8)
+            slot = ra.at[which, place, side]
             ar_copy(which, 0, step, slot, slot, g_peer(step)).wait_recv()
         total = None
-        for i in range(4):
-            for j in range(4):
+        for i in range(8):
+            for j in range(2):
                 total = ra[which, i, j] if total is None else total + ra[which, i, j]
-        rb[which, xl, parity] = total
+        rb[which, z // 2] = total
         for step in range(1, 4):
-            slot = rb.at[which, xl, parity]
+            slot = rb.at[which, z // 2]
             ar_copy(which, 1, step, slot, slot, q_peer(step)).start()
 
     def ar_third(which):
         for step in range(1, 4):
-            side, other = q_place(step)
-            slot = rb.at[which, side, other]
+            slot = rb.at[which, (z // 2 + 4 - step) % 4]
             ar_copy(which, 1, step, slot, slot, q_peer(step)).wait_recv()
-        total = (rb[which, 0, 0] + rb[which, 0, 1]) + (rb[which, 1, 0] + rb[which, 1, 1])
-        gc[which, y, zh // 2, zh % 2] = total
-        for step in range(1, 16):
-            slot = gc.at[which, y, zh // 2, zh % 2]
+        total = rb[which, 0]
+        for i in range(1, 4):
+            total = total + rb[which, i]
+        gc[which, m, parity] = total
+        for step in range(1, 16):
+            slot = gc.at[which, m, parity]
             ar_copy(which, 2, step, slot, slot, g_peer(step)).start()
 
     def ar_finish(which):
         for step in range(1, 16):
-            place, level = g_place(step, -1)
-            slot = gc.at[which, place, level // 2, level % 2]
+            place, side = g_place(-(step % 8) + 8, step // 8)
+            slot = gc.at[which, place, side]
             ar_copy(which, 2, step, slot, slot, g_peer(step)).wait_recv()
 
     def ar_settle(which):
-        slot = gc.at[which, 0, 0, 0]
+        slot = gc.at[which, 0, 0]
         for step in range(1, 16):
             ar_copy(which, 0, step, slot, slot, g_peer(step)).wait_send()
             ar_copy(which, 2, step, slot, slot, g_peer(step)).wait_send()
@@ -303,13 +291,13 @@
                     spread = jnp.where(columns == b * 4 + i, row, spread)
             for side in range(2):
                 lanes = slice(side * 128, side * 128 + 128)
-                sums[which, :, :, side, plane] = total[:, lanes].reshape(4, 2, 8, 128)
+                sums[which, :, side, plane] = total[:, lanes].reshape(8, 8, 128)
                 if plane == 2:
-                    sums[which, :, :, side, 3] = spread[:, lanes].reshape(4, 2, 8, 128)
+                    sums[which, :, side, 3] = spread[:, lanes].reshape(8, 8, 128)
 
     def totals(which, number):
         return jnp.concatenate(
-            [gc[which, :, :, side, number].reshape(64, 128) for side in range(2)], axis=1
+            [gc[which, :, side, number].reshape(64, 128) for side in range(2)], axis=1
         )
 
     def context_row(which, plane, i, whole):
@@ -367,7 +355,7 @@
             act = pre[plane, i] + gain_vec * context + time_col
             gate = jax.nn.sigmoid(act)
             values = rows[0, plane, 1 + i, h, k].astype(F32)
-            out_a[plane, i] = (values + act * gate).astype(BF16)
+            block_out[plane, i] = (values + act * gate).astype(BF16)
             grad = cot[plane, i].astype(F32) * gate * (1.0 + act * (1.0 - gate))
             rows[1, plane, 1 + i, h, k] = grad.astype(BF16)
             return carry
@@ -403,46 +391,48 @@
             part.append(jnp.zeros((32, 64), F32))
             block = jnp.concatenate(part, axis=1)
             for j in range(8):
-                wpack[j, pl.ds(i * 4, 4)] = block[j * 4 : j * 4 + 4]
-        wsend[...] = wpack[...].astype(WIRE)
+                wsend[j, i % 2, i // 2] = block[j * 4 : j * 4 + 4]
 
     def wg_start():
-        for step in range(1, 8):
-            wg_copy(0, step, wsend.at[(m + step) % 8], rz.at[m], m_peer(step)).start()
-        rz[m] = wsend[m]
+        for step in range(1, 16):
+            place, side = g_place(step % 8, step // 8)
+            wg_copy(0, step, wsend.at[place, side], rz.at[m, parity], g_peer(step)).start()
+        rz[m, parity] = wsend[m, parity]
 
     def wg_second():
-        for step in range(1, 8):
-            slot = rz.at[(m + 8 - step) % 8]
-            wg_copy(0, step, slot, slot, m_peer(step)).wait_recv()
-        total = rz[0].astype(F32)
-        for i in range(1, 8):
-            total = total + rz[i].astype(F32)
+        for step in range(1, 16):
+            place, side = g_place(-(step % 8) + 8, step // 8)
+            slot = rz.at[place, side]
+            wg_copy(0, step, slot, slot, g_peer(step)).wait_recv()
+        total = None
         for i in range(8):
-            rv[i] = total[i * 4 : i * 4 + 4]
-        for step in range(1, 8):
-            wg_copy(1, step, rv.at[(z + step) % 8], rm.at[z], z_peer(step)).start()
-        rm[z] = rv[z]
+            for j in range(2):
+                total = rz[i, j] if total is None else total + rz[i, j]
+        rv[...] = total
+        for step in range(1, 4):
+            wg_copy(1, step, rv.at[(z // 2 + step) % 4], rm.at[z // 2], q_peer(step)).start()
+        rm[z // 2] = rv[z // 2]
 
     def wg_finish():
-        for step in range(1, 8):
-            slot = rm.at[(z + 8 - step) % 8]
-            wg_copy(1, step, slot, slot, z_peer(step)).wait_recv()
+        for step in range(1, 4):
+            slot = rm.at[(z // 2 + 4 - step) % 4]
+            wg_copy(1, step, slot, slot, q_peer(step)).wait_recv()
         total = rm[0]
-        for i in range(1, 8):
+        for i in range(1, 4):
             total = total + rm[i]
         for tap in range(9):
             weight_grad[tap] = total[:, tap * 64 : tap * 64 + 64]
 
     def wg_settle():
-        for step in range(1, 8):
-            wg_copy(0, step, wsend.at[0], rz.at[0], m_peer(step)).wait_send()
-            wg_copy(1, step, rv.at[0], rm.at[0], z_peer(step)).wait_send()
+        for step in range(1, 16):
+            wg_copy(0, step, wsend.at[0, 0], rz.at[0, 0], g_peer(step)).wait_send()
+        for step in range(1, 4):
+            wg_copy(1, step, rv.at[0], rm.at[0], q_peer(step)).wait_send()
 
     def make_columns():
         ids = lax.broadcasted_iota(jnp.int32, (64, 128), 0) + p * 64
         columns_of[1] = time_embed(step_index[0], ids)[:, :1]
-        across_lanes = jnp.broadcast_to(gain[...].astype(F32).reshape(1, 64), (64, 64))
+        across_lanes = jnp.broadcast_to(gain_row[...].astype(F32).reshape(1, 64), (64, 64))
         same = lax.broadcasted_iota(jnp.int32, (64, 64), 0) == lax.broadcasted_iota(
             jnp.int32, (64, 64), 1
         )
@@ -455,7 +445,7 @@
         def finish_back(i, carry):
             context = context_row(1, plane, i, whole) * (1.0 / 256.0)
             grad = cot[plane, i].astype(F32) + pre[plane, i] + gain_vec * context
-            out_b[plane, i] = grad.astype(BF16)
+            input_grad[plane, i] = grad.astype(BF16)
             return carry
 
         lax.fori_loop(0, 4, finish_back, 0)
@@ -463,6 +453,7 @@
     for i in range(3):
         loads[i].wait()
     make_sums(0)
+    gain_load.wait()
     make_columns()
     zero_row = jnp.zeros((2, 2, 64, 256), BF16)
 
@@ -478,83 +469,106 @@
             for plane in range(3):
                 rows[which, plane, 5] = zero_row
 
+    arrived = wa.at[:, 1 - h, k]
+
+    def loaded():
+        for copy in loads[3:]:
+            copy.wait()
+        w_copy(1, wa.at[:, h, k], wa.at[:, h, k], beside).start()
+
+    def w_first():
+        w_copy(0, wo, wa.at[:, h, k], across).start()
+
+    def w_forward():
+        w_copy(0, arrived, arrived, across).wait_recv()
+        w_copy(2, arrived, arrived, beside).start()
+
+    def w_turn():
+        for kind, dst in ((1, wa.at[:, h, 1 - k]), (2, wa.at[:, 1 - h, 1 - k])):
+            w_copy(kind, dst, dst, beside).wait_recv()
+        turn_weights()
+
+    def convolve_step(which, plane):
+        convolve(which, plane, wb if which else wf, which == 1)
+
+    def weight_step(plane):
+        stack_plane(plane)
+        weight_terms(plane)
+
     meet()
     ar_start(0)
-    send_across(0, 0)
-    send_across(0, 1)
-    for plane in range(3):
-        send_near(0, plane)
-    for copy in loads[3:]:
-        copy.wait()
-    w_copy(1, wa.at[:, h, k], wa.at[:, h, k], beside).start()
+    send_edges(0, 0)
+    send_edges(0, 1)
+    send_edges(0, 2)
+    send_inner(0, 0)
+    send_inner(0, 1)
+    send_inner(0, 2)
+    send_near(0, 0)
+    send_near(0, 1)
+    send_near(0, 2)
+    loaded()
     pass_edges(0, 0)
     ar_second(0)
-    send_across(0, 2)
+    pass_edges(0, 1)
+    pass_edges(0, 2)
+    pass_rim(0, 0)
     pass_on(0, 0)
-    pass_edges(0, 1)
+    ar_third(0)
+    w_first()
+    pass_rim(0, 1)
     pass_on(0, 1)
-    pass_rim(0, 0)
     arrive(0, 0)
-    convolve(0, 0, wf, False)
-    ar_third(0)
-    pass_edges(0, 2)
+    convolve_step(0, 0)
+    pass_rim(0, 2)
     pass_on(0, 2)
-    w_copy(0, wo, wa.at[:, h, k], across).start()
-    pass_rim(0, 1)
     arrive(0, 1)
-    convolve(0, 1, wf, False)
-    pass_rim(0, 2)
+    convolve_step(0, 1)
     arrive(0, 2)
-    convolve(0, 2, wf, False)
-
+    convolve_step(0, 2)
     ar_finish(0)
     finish_plane(0)
-    send_across(1, 0)
+    send_edges(1, 0)
     finish_plane(1)
-    send_across(1, 1)
+    send_edges(1, 1)
     finish_plane(2)
+    send_edges(1, 2)
     make_sums(1)
     ar_start(1)
-    for plane in range(3):
-        send_near(1, plane)
-        pltpu.make_async_copy(out_a.at[plane], block_out.at[plane], store_sem.at[0, plane]).start()
-    stack_plane(0)
-    weight_terms(0)
+    send_near(1, 0)
+    send_near(1, 1)
+    send_near(1, 2)
+    send_inner(1, 0)
+    send_inner(1, 1)
+    send_inner(1, 2)
+    weight_step(0)
     pass_edges(1, 0)
-    stack_plane(1)
-    weight_terms(1)
-    pass_on(1, 0)
+    weight_step(1)
     pass_edges(1, 1)
-    stack_plane(2)
-    weight_terms(2)
+    weight_step(2)
     ar_second(1)
-    send_across(1, 2)
-    pass_on(1, 1)
+    pass_edges(1, 2)
     wg_pack()
     wg_start()
     pass_rim(1, 0)
-    arrived = wa.at[:, 1 - h, k]
-    w_copy(0, arrived, arrived, across).wait_recv()
-    w_copy(2, arrived, arrived, beside).start()
-    pass_edges(1, 2)
+    pass_on(1, 0)
+    w_forward()
+    w_turn()
     ar_third(1)
+    pass_rim(1, 1)
+    pass_on(1, 1)
+    arrive(1, 0)
+    convolve_step(1, 0)
+    pass_rim(1, 2)
     pass_on(1, 2)
-    for kind, dst in ((1, wa.at[:, h, 1 - k]), (2, wa.at[:, 1 - h, 1 - k])):
-        w_copy(kind, dst, dst, beside).wait_recv()
-    turn_weights()
-    pass_rim(1, 1)
-    arrive(1, 0)
-    convolve(1, 0, wb, True)
-    pass_rim(1, 2)
     arrive(1, 1)
-    convolve(1, 1, wb, True)
+    convolve_step(1, 1)
     wg_second()
     arrive(1, 2)
-    convolve(1, 2, wb, True)
+    convolve_step(1, 2)
     ar_finish(1)
-    for plane in range(3):
-        finish_back_plane(plane)
-        pltpu.make_async_copy(out_b.at[plane], input_grad.at[plane], store_sem.at[1, plane]).start()
+    finish_back_plane(0)
+    finish_back_plane(1)
+    finish_back_plane(2)
     wg_finish()
 
     for which in range(2):
@@ -565,21 +579,14 @@
     for kind in (1, 2):
         w_copy(kind, arrived, arrived, beside).wait_send()
     wg_settle()
-    for plane in range(3):
-        pltpu.make_async_copy(out_a.at[plane], block_out.at[plane], store_sem.at[0, plane]).wait()
-        pltpu.make_async_copy(out_b.at[plane], input_grad.at[plane], store_sem.at[1, plane]).wait()
 
 
 def place(*refs):
-    sources, targets, held, sems = refs[:3], refs[3:6], refs[6:9], refs[9]
-    arriving = [pltpu.make_async_copy(sources[i], held[i], sems.at[0, i]) for i in range(3)]
-    leaving = [pltpu.make_async_copy(held[i], targets[i], sems.at[1, i]) for i in range(3)]
-    for copy in arriving:
+    sources, targets, sems = refs[:3], refs[3:6], refs[6]
+    copies = [pltpu.make_async_copy(sources[i], targets[i], sems.at[i]) for i in range(3)]
+    for copy in copies:
         copy.start()
-    for i in range(3):
-        arriving[i].wait()
-        leaving[i].start()
-    for copy in leaving:
+    for copy in copies:
         copy.wait()
 
 
@@ -594,13 +601,17 @@
         jax.ShapeDtypeStruct((3, 4, 64, 256), BF16),
         jax.ShapeDtypeStruct((9, 4, 64), F32),
     )
+    def held(array):
+        return pltpu.with_memory_space_constraint(array, pltpu.HBM)
+
     results = pl.pallas_call(
         kernel,
         out_shape=shapes,
-        in_specs=[hbm, hbm, hbm, vmem, smem],
-        out_specs=(anywhere, anywhere, vmem),
+        in_specs=[hbm, hbm, hbm, hbm, smem],
+        out_specs=(vmem, vmem, vmem),
         scratch_shapes=[
             pltpu.VMEM((2, 64, 1), F32),
+            pltpu.VMEM((64,), BF16),
             pltpu.VMEM((2, 3, 6, 2, 2, 64, 256), BF16),
             pltpu.VMEM((3, 4, 64, 256), BF16),
             pltpu.VMEM((192, 768), BF16),
@@ -609,42 +620,38 @@
             pltpu.VMEM((9, 64, 128), BF16),
             pltpu.VMEM((3, 4, 64, 256), F32),
             pltpu.VMEM((3, 4, 192, 256), BF16),
-            pltpu.VMEM((3, 4, 64, 256), BF16),
-            pltpu.VMEM((3, 4, 64, 256), BF16),
-            pltpu.VMEM((2, 4, 2, 2, 4, 8, 128), F32),
+            pltpu.VMEM((2, 8, 2, 4, 8, 128), F32),
             pltpu.VMEM((2, 2, 4, 64, 1), F32),
-            pltpu.VMEM((2, 4, 4, 4, 8, 128), F32),
-            pltpu.VMEM((2, 2, 2, 4, 8, 128), F32),
-            pltpu.VMEM((2, 4, 2, 2, 4, 8, 128), F32),
+            pltpu.VMEM((2, 8, 2, 4, 8, 128), F32),
+            pltpu.VMEM((2, 4, 4, 8, 128), F32),
+            pltpu.VMEM((2, 8, 2, 4, 8, 128), F32),
             pltpu.VMEM((3, 256, 192), F32),
-            pltpu.VMEM((8, 32, 640), F32),
-            pltpu.VMEM((8, 32, 640), WIRE),
-            pltpu.VMEM((8, 32, 640), WIRE),
-            pltpu.VMEM((8, 4, 640), F32),
-            pltpu.VMEM((8, 4, 640), F32),
-            dma((15,)),
+            pltpu.VMEM((8, 2, 4, 4, 640), F32),
+            pltpu.VMEM((8, 2, 4, 4, 640), F32),
+            pltpu.VMEM((4, 4, 640), F32),
+            pltpu.VMEM((4, 4, 640), F32),
+            dma((16,)),
             dma((2, 3, 11)),
             dma((2, 3, 11)),
             dma((2, 3, 15)),
             dma((2, 3, 15)),
             dma((3,)),
             dma((3,)),
-            dma((2, 7)),
-            dma((2, 7)),
-            dma((2, 3)),
+            dma((2, 15)),
+            dma((2, 15)),
         ],
         compiler_params=pltpu.CompilerParams(
             collective_id=0, has_side_effects=True, vmem_limit_bytes=VMEM_LIMIT
         ),
         name="triplane",
-    )(planes, cotangent, conv_weight, context_gain, step_index)
+    )(held(planes), held(cotangent), held(conv_weight), held(context_gain), step_index)
     block_out, input_grad, weight_grad = pl.pallas_call(
         place,
         out_shape=shapes,
-        in_specs=[anywhere] * 3,
+        in_specs=[vmem] * 3,
         out_specs=(hbm, hbm, hbm),
-        scratch_shapes=[pltpu.VMEM(shape.shape, shape.dtype) for shape in shapes] + [dma((2, 3))],
-        compiler_params=pltpu.CompilerParams(vmem_limit_bytes=VMEM_LIMIT),
+        scratch_shapes=[dma((3,))],
+        compiler_params=pltpu.CompilerParams(vmem_limit_bytes=32 * 1024 * 1024),
         name="place",
     )(*results)
     return block_out, input_grad, jnp.transpose(weight_grad, (0, 2, 1))

time: 74.5 us -> 70.2 us (0.942)
  Pallas kernels: 72.7 us -> 68.8 us
    pallas_call x2, Pallas kernels: 72.7 us -> 68.8 us  [the longest x1 67.9 us: on_device(): pl.pallas_call(kernel, out_shape=shapes, in_specs=[hbm, hbm, hbm, hbm, sm...]
where the time goes in v3:
time: 70.2 us; the launch traced here: 70.1 us
  Pallas kernels  68.8 us (98%)
  between operations  1.29 us (2%)
    pallas_call x1, Pallas kernels, on_device(): pl.pallas_call(kernel, out_shape=shapes, in_specs=[hbm, hbm, hbm, hbm, sm...  67.9 us

profile of v3, /device:TPU:2, one launch (start us, length us, event | category | flops | bytes accessed | tf_op | source)
XLA Modules:
  0.0 70.1 jit_solution(4174221267072497298)
XLA Ops:
  1.3 67.9 %triplane.1 = (bf16[3,4,64,256]{3,2,1,0:T(8,128)(2,1)S(1)}, bf16[3,4,64,256]{3,2,1,0:T(8,128)(2,1)S(1)}, f32[9,4,64]{2,1,0:T(4,128)S(1)}) custom-call(bf16[3,4,64,256]{3,2,1,0:T(8,128)(2,1)} %planes.1, bf16[3,4,64,256]{3,2,1,0:T(8,128)(2,1)} %cotangent.1, bf16[9,64,256]{2,1,0:T(8,128)(2,1)} %weights.1, bf16[64]{0:T(256)(128)(2,1)} %gain.1, s32[1]{0:T(128)S(6)} %copy.8.step_index), custom_call_target="tpu_custom_call" | custom-call | tf_op jit(solution)/shard_map/triplane/pallas_call | solution.py:607
  69.2 0.9 %place.1 = (bf16[3,4,64,256]{3,2,1,0:T(8,128)(2,1)}, bf16[3,4,64,256]{3,2,1,0:T(8,128)(2,1)}, f32[9,4,64]{2,1,0:T(4,128)}) custom-call(bf16[3,4,64,256]{3,2,1,0:T(8,128)(2,1)S(1)} %get-tuple-element.9.refs_0_, bf16[3,4,64,256]{3,2,1,0:T(8,128)(2,1)S(1)} %get-tuple-element.10.refs_1_, f32[9,4,64]{2,1,0:T(4,128)S(1)} %get-tuple-element.11.refs_2_), custom_call_target="tpu_custom_call" | custom-call | tf_op jit(solution)/shard_map/place/pallas_call | solution.py:648

commit v4 on v3

--- a/solution.py
+++ b/solution.py
@@ -35,7 +35,7 @@
     planes, cotangent, weights, gain, step_index,
     block_out, input_grad, weight_grad,
     columns_of, gain_row, rows, cot, wf, wa, wb, wo, pre, stacks,
-    sums, row_sums, ra, rb, gc,
+    sums, row_sums, ra, rb, gc, sumsb, rab, gcb,
     wacc, wsend, rz, rv, rm,
     load_sem, send_sem, recv_sem, ar_send, ar_recv, w_send, w_recv, wg_send, wg_recv,
 ):
@@ -227,24 +227,38 @@
             device_id_type=MESH,
         )
 
+    def first_slot(which, place, side):
+        return ra.at[which, place, side] if which == 0 else rab.at[place, side]
+
+    def last_slot(which, place, side):
+        return gc.at[which, place, side] if which == 0 else gcb.at[place, side]
+
     def ar_start(which):
+        if which == 1:
+            sumsb[...] = sums[1].reshape(8, 2, 32, 128).astype(BF16)
         for step in range(1, 16):
             place, side = g_place(step % 8, step // 8)
             ar_copy(
-                which, 0, step, sums.at[which, place, side], ra.at[which, m, parity], g_peer(step)
+                which, 0, step,
+                sums.at[which, place, side] if which == 0 else sumsb.at[place, side],
+                first_slot(which, m, parity), g_peer(step),
             ).start()
-        ra[which, m, parity] = sums[which, m, parity]
+        if which == 0:
+            ra[which, m, parity] = sums[which, m, parity]
+        else:
+            rab[m, parity] = sumsb[m, parity]
 
     def ar_second(which):
         for step in range(1, 16):
             place, side = g_place(-(step % 8) + 8, step // 8)
-            slot = ra.at[which, place, side]
+            slot = first_slot(which, place, side)
             ar_copy(which, 0, step, slot, slot, g_peer(step)).wait_recv()
         total = None
         for i in range(8):
             for j in range(2):
-                total = ra[which, i, j] if total is None else total + ra[which, i, j]
-        rb[which, z // 2] = total
+                term = ra[which, i, j] if which == 0 else rab[i, j].astype(F32)
+                total = term if total is None else total + term
+        rb[which, z // 2] = total.reshape(4, 8, 128)
         for step in range(1, 4):
             slot = rb.at[which, z // 2]
             ar_copy(which, 1, step, slot, slot, q_peer(step)).start()
@@ -256,22 +270,26 @@
         total = rb[which, 0]
         for i in range(1, 4):
             total = total + rb[which, i]
-        gc[which, m, parity] = total
-        for step in range(1, 16):
-            slot = gc.at[which, m, parity]
+        if which == 0:
+            gc[which, m, parity] = total
+        else:
+            gcb[m, parity] = total.reshape(32, 128).astype(BF16)
+        for step in range(1, 16):
+            slot = last_slot(which, m, parity)
             ar_copy(which, 2, step, slot, slot, g_peer(step)).start()
 
     def ar_finish(which):
         for step in range(1, 16):
             place, side = g_place(-(step % 8) + 8, step // 8)
-            slot = gc.at[which, place, side]
+            slot = last_slot(which, place, side)
             ar_copy(which, 2, step, slot, slot, g_peer(step)).wait_recv()
 
     def ar_settle(which):
-        slot = gc.at[which, 0, 0]
-        for step in range(1, 16):
-            ar_copy(which, 0, step, slot, slot, g_peer(step)).wait_send()
-            ar_copy(which, 2, step, slot, slot, g_peer(step)).wait_send()
+        ends = last_slot(which, 0, 0)
+        slot = rb.at[which, 0]
+        for step in range(1, 16):
+            ar_copy(which, 0, step, ends, ends, g_peer(step)).wait_send()
+            ar_copy(which, 2, step, ends, ends, g_peer(step)).wait_send()
         for step in range(1, 4):
             ar_copy(which, 1, step, slot, slot, q_peer(step)).wait_send()
 
@@ -296,9 +314,12 @@
                     sums[which, :, side, 3] = spread[:, lanes].reshape(8, 8, 128)
 
     def totals(which, number):
-        return jnp.concatenate(
-            [gc[which, :, side, number].reshape(64, 128) for side in range(2)], axis=1
-        )
+        if which == 0:
+            halves = [gc[which, :, side, number] for side in range(2)]
+        else:
+            at = slice(number * 8, number * 8 + 8)
+            halves = [gcb[:, side].astype(F32)[:, at, :] for side in range(2)]
+        return jnp.concatenate([half_of.reshape(64, 128) for half_of in halves], axis=1)
 
     def context_row(which, plane, i, whole):
         if plane == 0:
@@ -563,11 +584,11 @@
     arrive(1, 1)
     convolve_step(1, 1)
     wg_second()
-    arrive(1, 2)
-    convolve_step(1, 2)
     ar_finish(1)
     finish_back_plane(0)
     finish_back_plane(1)
+    arrive(1, 2)
+    convolve_step(1, 2)
     finish_back_plane(2)
     wg_finish()
 
@@ -625,6 +646,9 @@
             pltpu.VMEM((2, 8, 2, 4, 8, 128), F32),
             pltpu.VMEM((2, 4, 4, 8, 128), F32),
             pltpu.VMEM((2, 8, 2, 4, 8, 128), F32),
+            pltpu.VMEM((8, 2, 32, 128), BF16),
+            pltpu.VMEM((8, 2, 32, 128), BF16),
+            pltpu.VMEM((8, 2, 32, 128), BF16),
             pltpu.VMEM((3, 256, 192), F32),
             pltpu.VMEM((8, 2, 4, 4, 640), F32),
             pltpu.VMEM((8, 2, 4, 4, 640), F32),

time: 70.2 us -> 68.2 us (0.972)
  Pallas kernels: 68.8 us -> 66.7 us
    pallas_call x1, Pallas kernels: 67.9 us -> 65.8 us  [on_device(): pl.pallas_call(kernel, out_shape=shapes, in_specs=[hbm, hbm, hbm, hbm, sm...]
where the time goes in v4:
time: 68.2 us; the launch traced here: 68 us
  Pallas kernels  66.7 us (98%)
  between operations  1.29 us (2%)
    pallas_call x1, Pallas kernels, on_device(): pl.pallas_call(kernel, out_shape=shapes, in_specs=[hbm, hbm, hbm, hbm, sm...  65.8 us

profile of v4, /device:TPU:2, one launch (start us, length us, event | category | flops | bytes accessed | tf_op | source)
XLA Modules:
  0.0 68.0 jit_solution(12576846684346116457)
XLA Ops:
  1.3 65.8 %triplane.1 = (bf16[3,4,64,256]{3,2,1,0:T(8,128)(2,1)S(1)}, bf16[3,4,64,256]{3,2,1,0:T(8,128)(2,1)S(1)}, f32[9,4,64]{2,1,0:T(4,128)S(1)}) custom-call(bf16[3,4,64,256]{3,2,1,0:T(8,128)(2,1)} %planes.1, bf16[3,4,64,256]{3,2,1,0:T(8,128)(2,1)} %cotangent.1, bf16[9,64,256]{2,1,0:T(8,128)(2,1)} %weights.1, bf16[64]{0:T(256)(128)(2,1)} %gain.1, s32[1]{0:T(128)S(6)} %copy.8.step_index), custom_call_target="tpu_custom_call" | custom-call | tf_op jit(solution)/shard_map/triplane/pallas_call | solution.py:628
  67.1 0.9 %place.1 = (bf16[3,4,64,256]{3,2,1,0:T(8,128)(2,1)}, bf16[3,4,64,256]{3,2,1,0:T(8,128)(2,1)}, f32[9,4,64]{2,1,0:T(4,128)}) custom-call(bf16[3,4,64,256]{3,2,1,0:T(8,128)(2,1)S(1)} %get-tuple-element.9.refs_0_, bf16[3,4,64,256]{3,2,1,0:T(8,128)(2,1)S(1)} %get-tuple-element.10.refs_1_, f32[9,4,64]{2,1,0:T(4,128)S(1)} %get-tuple-element.11.refs_2_), custom_call_target="tpu_custom_call" | custom-call | tf_op jit(solution)/shard_map/place/pallas_call | solution.py:672

commit v5 on v4

--- a/solution.py
+++ b/solution.py
@@ -550,11 +550,11 @@
     finish_plane(0)
     send_edges(1, 0)
     finish_plane(1)
-    send_edges(1, 1)
     finish_plane(2)
-    send_edges(1, 2)
     make_sums(1)
     ar_start(1)
+    send_edges(1, 1)
+    send_edges(1, 2)
     send_near(1, 0)
     send_near(1, 1)
     send_near(1, 2)

time: 68.2 us -> 68.4 us (level)
  no operation moved by 1% of the time
where the time goes in v5:
time: 68.4 us; the launch traced here: 68.3 us
  Pallas kernels  67 us (98%)
  between operations  1.29 us (2%)
    pallas_call x1, Pallas kernels, on_device(): pl.pallas_call(kernel, out_shape=shapes, in_specs=[hbm, hbm, hbm, hbm, sm...  66.1 us

profile of v5, /device:TPU:2, one launch (start us, length us, event | category | flops | bytes accessed | tf_op | source)
XLA Modules:
  0.0 68.3 jit_solution(11049606116649123624)
XLA Ops:
  1.3 66.1 %triplane.1 = (bf16[3,4,64,256]{3,2,1,0:T(8,128)(2,1)S(1)}, bf16[3,4,64,256]{3,2,1,0:T(8,128)(2,1)S(1)}, f32[9,4,64]{2,1,0:T(4,128)S(1)}) custom-call(bf16[3,4,64,256]{3,2,1,0:T(8,128)(2,1)} %planes.1, bf16[3,4,64,256]{3,2,1,0:T(8,128)(2,1)} %cotangent.1, bf16[9,64,256]{2,1,0:T(8,128)(2,1)} %weights.1, bf16[64]{0:T(256)(128)(2,1)} %gain.1, s32[1]{0:T(128)S(6)} %copy.8.step_index), custom_call_target="tpu_custom_call" | custom-call | tf_op jit(solution)/shard_map/triplane/pallas_call | solution.py:628
  67.4 0.9 %place.1 = (bf16[3,4,64,256]{3,2,1,0:T(8,128)(2,1)}, bf16[3,4,64,256]{3,2,1,0:T(8,128)(2,1)}, f32[9,4,64]{2,1,0:T(4,128)}) custom-call(bf16[3,4,64,256]{3,2,1,0:T(8,128)(2,1)S(1)} %get-tuple-element.9.refs_0_, bf16[3,4,64,256]{3,2,1,0:T(8,128)(2,1)S(1)} %get-tuple-element.10.refs_1_, f32[9,4,64]{2,1,0:T(4,128)S(1)} %get-tuple-element.11.refs_2_), custom_call_target="tpu_custom_call" | custom-call | tf_op jit(solution)/shard_map/place/pallas_call | solution.py:672
